TPU v7x, 512 devices: a whole 4x8x8 slice. The times are simulated.
512 devices in a mesh: elec: 64 (over x, y, core), therm: 8 (over z).
Axes of the slice: x: 4, y: 8, z: 8, core: 2. Of those that a mesh axis runs over, the one named last changes fastest.
Arguments:
- injected_amperage: bfloat16 [16384, 64, 128], P(('elec', 'therm')), may hold values from -6 to 6
- voltage_self_admittance: float32 [16384, 64], P(('elec', 'therm')), may hold values from 1.2 to 2.5
- voltage_coupling_tiles: bfloat16 [16384, 4, 64, 64], P(('elec', 'therm')), may hold values from -0.5 to 0.5
- voltage_partner_tile_ids: int32 [16384, 4], P(('elec', 'therm')), may hold values from 0 to 31
- interface_tiles_per_level: int32 [2048, 2], P(('elec', 'therm')), may hold values from 0 to 31
- interface_admittance: bfloat16 [4096, 64, 64], P(('elec', 'therm')), may hold values from -0.5 to 0.5
- warmth_receiver_layer: int32 [16384, 1], P(('elec', 'therm')), may hold values from 0 to 7; in each aligned block of 32 rows (0 to 31, 32 to 63, ...) at most 8 rows name the same one
- warmth_receiver_tile: int32 [16384], P(('elec', 'therm')), may hold values from 0 to 31
- warmth_values: bfloat16 [16384, 64, 128], P(('elec', 'therm')), may hold values from -4 to 4
- warmth_self_coefficient: float32 [16384, 64], P(('elec', 'therm')), may hold values from 1 to 3
- warmth_coupling_tiles: bfloat16 [16384, 3, 64, 64], P(('elec', 'therm')), may hold values from -0.4375 to 0.4375
- warmth_partner_tile_ids: int32 [16384, 3], P(('elec', 'therm')), may hold values from 0 to 31
- layer_boundary_couplings: bfloat16 [2048, 64, 64], P(('elec', 'therm')), may hold values from -0.4375 to 0.4375
- substance_kind: int32 [16384, 64], P(('elec', 'therm')), may hold values from 0 to 7
- reference_material_kappas: float32 [8], replicated, may hold values from 0.5 to 4
- warmth_storage_per_point: float32 [16384, 64], P(('elec', 'therm')), may hold values from 1 to 4
Outputs:
- voltage_solution: bfloat16 [16384, 64, 128], P(('elec', 'therm'))
- advanced_warmth_values: float32 [16384, 64, 128], P(('elec', 'therm'))
Inputs may be any that keep to these rules, and one draw needn't show every extreme that they name: `warmth_receiver_layer`: among the 32 blocks of one device at most 8 name the same owner, and exactly 8 do for some owner. `voltage_partner_tile_ids`: indexes a block of the same device. `interface_tiles_per_level`: indexes a block of the same device. `warmth_receiver_tile`: indexes a thermal block of the owner. `warmth_partner_tile_ids`: indexes a thermal block of the same device.
All inputs are finite; a program needn't handle non-finite values.
Results may differ from a plain program's by a relative error of at most 0.025.
Values may be sent and summed in bfloat16 or wider, within the bound.
A program may use at most 64 MiB of HBM per device.

v0:
```python
import jax
import jax.numpy as jnp
from jax import lax
from jax.sharding import PartitionSpec as P

SWEEPS = 5
ZB = 2
relax_factor = 0.8
time_increment = 0.5


def from_partner(block, axis, bit):
    count = lax.axis_size(axis)
    route = []
    for low in range(count):
        high = low | 1 << bit
        if high != low and high < count:
            route += [(low, high), (high, low)]
    return lax.ppermute(block, axis, route)


def with_halo(x, sides, width):
    for axis, dim in sides:
        size, length = (lax.axis_size(axis), x.shape[dim])
        up = [(i, (i + 1) % size) for i in range(size - 1)]
        down = [(j, i) for i, j in up]
        last = lax.slice_in_dim(x, length - width, length, axis=dim)
        first = lax.slice_in_dim(x, 0, width, axis=dim)
        before = lax.ppermute(last, axis, up)
        after = lax.ppermute(first, axis, down)
        x = jnp.concatenate([before, x, after], axis=dim)
    return x


def near_product(field_b, near_blocks, near_index):
    picked = field_b[near_index]
    return jnp.einsum("rkab,rkbc->rac", near_blocks, picked, preferred_element_type=jnp.float32)


def electric_apply(
    field_b,
    voltage_self_admittance,
    voltage_coupling_tiles,
    voltage_partner_tile_ids,
    interface_tiles_per_level,
    interface_admittance,
):
    total = voltage_self_admittance[:, :, None] * field_b.astype(jnp.float32) + near_product(
        field_b, voltage_coupling_tiles, voltage_partner_tile_ids
    )
    received = []
    for level_bit in range(interface_tiles_per_level.shape[0]):
        outgoing = field_b[interface_tiles_per_level[level_bit]]
        received.append(from_partner(outgoing, "elec", level_bit))
    incoming = jnp.concatenate(received, axis=0)
    face_terms = jnp.einsum(
        "sab,sbc->sac", interface_admittance, incoming, preferred_element_type=jnp.float32
    )
    targets = interface_tiles_per_level.reshape(-1)
    selector = (targets[None, :] == jnp.arange(field_b.shape[0])[:, None]).astype(jnp.float32)
    spread = jnp.dot(
        selector, face_terms.reshape(face_terms.shape[0], -1), precision=lax.Precision.HIGHEST
    )
    return total + spread.reshape(total.shape)


def body(
    injected_amperage,
    voltage_self_admittance,
    voltage_coupling_tiles,
    voltage_partner_tile_ids,
    interface_tiles_per_level,
    interface_admittance,
    warmth_receiver_layer,
    warmth_receiver_tile,
    warmth_values,
    warmth_self_coefficient,
    warmth_coupling_tiles,
    warmth_partner_tile_ids,
    layer_boundary_couplings,
    substance_kind,
    reference_material_kappas,
    warmth_storage_per_point,
):
    source = injected_amperage.astype(jnp.float32)
    potential_f = relax_factor * source / voltage_self_admittance[:, :, None]
    for sweep_index in range(SWEEPS - 1):
        field_b = potential_f.astype(jnp.bfloat16)
        image = electric_apply(
            field_b,
            voltage_self_admittance,
            voltage_coupling_tiles,
            voltage_partner_tile_ids,
            interface_tiles_per_level,
            interface_admittance,
        )
        potential_f = (
            potential_f + relax_factor * (source - image) / voltage_self_admittance[:, :, None]
        )
    voltage_solution = potential_f.astype(jnp.bfloat16)
    current = electric_apply(
        voltage_solution,
        voltage_self_admittance,
        voltage_coupling_tiles,
        voltage_partner_tile_ids,
        interface_tiles_per_level,
        interface_admittance,
    )
    heat_b = (voltage_solution.astype(jnp.float32) * current).astype(jnp.bfloat16)
    owners = warmth_receiver_layer[:, 0]
    warmth_tile_count = warmth_values.shape[0]
    block_ids = jnp.arange(warmth_tile_count)[:, None]
    own_index = lax.axis_index("therm")
    heat_piece = lax.all_gather(heat_b, "therm", axis=0, tiled=True)
    owner_piece = lax.all_gather(owners, "therm", axis=0, tiled=True)
    row_piece = lax.all_gather(warmth_receiver_tile, "therm", axis=0, tiled=True)
    selector = ((row_piece[None, :] == block_ids) & (owner_piece[None, :] == own_index)).astype(
        jnp.bfloat16
    )
    resistive_dissipation = jnp.einsum(
        "jr,rbc->jbc", selector, heat_piece, preferred_element_type=jnp.float32
    )
    warmth_distribution = warmth_values.astype(jnp.float32)
    material_hits = (
        substance_kind[:, :, None] == jnp.arange(reference_material_kappas.shape[0])[None, None, :]
    ).astype(jnp.float32)
    pass_along = jnp.sum(material_hits * reference_material_kappas[None, None, :], axis=2)
    diffusivity_coefficient = pass_along[:, :, None] * (1.0 + 0.4 * jnp.tanh(warmth_distribution))
    stream_flow_second = (diffusivity_coefficient * warmth_distribution).astype(jnp.bfloat16)
    padded = with_halo(stream_flow_second, (("therm", 0),), ZB)
    below = padded[:ZB]
    above = padded[padded.shape[0] - ZB :]
    warmth_spread_operator = warmth_self_coefficient[:, :, None] * stream_flow_second.astype(
        jnp.float32
    ) + near_product(stream_flow_second, warmth_coupling_tiles, warmth_partner_tile_ids)
    low_terms = jnp.einsum(
        "zab,zbc->zac", layer_boundary_couplings[:ZB], below, preferred_element_type=jnp.float32
    )
    high_terms = jnp.einsum(
        "zab,zbc->zac", layer_boundary_couplings[ZB:], above, preferred_element_type=jnp.float32
    )
    warmth_spread_operator = (
        warmth_spread_operator.at[:ZB].add(low_terms).at[warmth_tile_count - ZB :].add(high_terms)
    )
    advanced_warmth_values = (
        warmth_distribution
        + time_increment
        * (resistive_dissipation - warmth_spread_operator)
        / warmth_storage_per_point[:, :, None]
    )
    return (voltage_solution, advanced_warmth_values)


def solution(mesh):
    return jax.shard_map(
        body,
        mesh=mesh,
        in_specs=(
            P(("elec", "therm"), None, None),
            P(("elec", "therm"), None),
            P(("elec", "therm"), None, None, None),
            P(("elec", "therm"), None),
            P(("elec", "therm"), None),
            P(("elec", "therm"), None, None),
            P(("elec", "therm"), None),
            P(("elec", "therm")),
            P(("elec", "therm"), None, None),
            P(("elec", "therm"), None),
            P(("elec", "therm"), None, None, None),
            P(("elec", "therm"), None),
            P(("elec", "therm"), None, None),
            P(("elec", "therm"), None),
            P(),
            P(("elec", "therm"), None),
        ),
        out_specs=(P(("elec", "therm"), None, None), P(("elec", "therm"), None, None)),
        check_vma=False,
    )
```

profile of v0, /device:TPU:1, one launch (start us, length us, event | category | flops | bytes accessed | tf_op | source)
XLA Modules:
  0.0 201.4 jit_solution(17127404310122124780)
XLA Ops:
  7.2 1.1 slice_reduce_fusion.3
  8.3 1.4 fusion.40
  9.7 0.6 gather_fusion.4
  10.3 8.3 %collective-permute-start.3 = (bf16[2,64,128]{2,1,0:T(8,128)(2,1)S(1)}, bf16[2,64,128]{2,1,0:T(8,128)(2,1)S(1)}, u32[]{:S(2)}, u32[]{:S(2)}) collective-permute-start(bf16[2,64,128]{2,1,0:T(8,128)(2,1)S(1)} %gather_fusion.4), channel_id=1, source_target_pairs={{0,64},{64,0},{8,72},{72,8},{16,80},{80,16},{24,88},{88,24},{32,96... | collective-permute-start | bytes 98312 | tf_op jit(solution)/shard_map/ppermute | solution.py:19
  18.6 0.6 gather_fusion.3
  19.2 2.4 %collective-permute-start.2 = (bf16[2,64,128]{2,1,0:T(8,128)(2,1)S(1)}, bf16[2,64,128]{2,1,0:T(8,128)(2,1)S(1)}, u32[]{:S(2)}, u32[]{:S(2)}) collective-permute-start(bf16[2,64,128]{2,1,0:T(8,128)(2,1)S(1)} %gather_fusion.3), channel_id=1, source_target_pairs={{0,32},{32,0},{8,40},{40,8},{16,48},{48,16},{24,56},{56,24},{64,96... | collective-permute-start | bytes 98312 | tf_op jit(solution)/shard_map/ppermute | solution.py:19
  21.6 0.6 gather_fusion.2
  22.2 2.3 %collective-permute-start.1 = (bf16[2,64,128]{2,1,0:T(8,128)(2,1)S(1)}, bf16[2,64,128]{2,1,0:T(8,128)(2,1)S(1)}, u32[]{:S(2)}, u32[]{:S(2)}) collective-permute-start(bf16[2,64,128]{2,1,0:T(8,128)(2,1)S(1)} %gather_fusion.2), channel_id=1, source_target_pairs={{0,16},{16,0},{8,24},{24,8},{32,48},{48,32},{40,56},{56,40},{64,80... | collective-permute-start | bytes 98312 | tf_op jit(solution)/shard_map/ppermute | solution.py:19
  24.5 0.6 gather_fusion.1
  25.1 3.4 %collective-permute-start = (bf16[2,64,128]{2,1,0:T(8,128)(2,1)S(1)}, bf16[2,64,128]{2,1,0:T(8,128)(2,1)S(1)}, u32[]{:S(2)}, u32[]{:S(2)}) collective-permute-start(bf16[2,64,128]{2,1,0:T(8,128)(2,1)S(1)} %gather_fusion.1), channel_id=1, source_target_pairs={{0,8},{8,0},{16,24},{24,16},{32,40},{40,32},{48,56},{56,48},{64,72... | collective-permute-start | bytes 98312 | tf_op jit(solution)/shard_map/ppermute | solution.py:19
  28.5 0.7 compare_select_fusion.1
  29.4 0.8 copy.74
  30.2 2.2 %gather_fusion = bf16[128,64,128]{2,1,0:T(8,128)(2,1)} fusion(bf16[32,64,128]{2,1,0:T(8,128)(2,1)S(1)} %fusion.40, s32[1024]{0:T(1024)S(1)} %pad_clamp_fusion.5), kind=kCustom, calls=%fused_computation | custom fusion | bytes 4194816 | tf_op jit(solution)/shard_map/gather | solution.py:36
  32.6 0.7 fusion.49
  33.3 4.2 %fusion.120 = (bf16[32,64,128]{2,1,0:T(8,128)(2,1)S(1)}, f32[32,64,128]{2,1,0:T(8,128)}) fusion(f32[32,64,128]{2,0,1:T(8,128)S(1)} %fusion.49, bf16[32,4,64,64]{3,2,1,0:T(8,128)(2,1)S(1)} %copy-done, bf16[32,4,64,128]{3,2,1,0:T(8,128)(2,1)} %bitcast.203, f32[32,64]{1,0:T(8,128)S(1)} %copy-done.3, bf16[32,64,128]{2,1,0:T(8,128)(2,1)} %param.20), kind=kOutput, calls=%fused_computation.184 | convolution fusion | flops 137625600 | bytes 6299648 | tf_op jit(solution)/shard_map/rkab,rkbc->rac/dot_general | solution.py:37
  38.1 0.6 gather_fusion.8
  38.7 0.6 gather_fusion.7
  39.2 0.6 gather_fusion.6
  39.8 5.7 %collective-permute-start.7 = (bf16[2,64,128]{2,1,0:T(8,128)(2,1)S(1)}, bf16[2,64,128]{2,1,0:T(8,128)(2,1)S(1)}, u32[]{:S(2)}, u32[]{:S(2)}) collective-permute-start(bf16[2,64,128]{2,1,0:T(8,128)(2,1)S(1)} %gather_fusion.9), channel_id=1, source_target_pairs={{0,64},{64,0},{8,72},{72,8},{16,80},{80,16},{24,88},{88,24},{32,96... | collective-permute-start | bytes 98312 | tf_op jit(solution)/shard_map/ppermute | solution.py:19
  45.4 4.5 %collective-permute-start.6 = (bf16[2,64,128]{2,1,0:T(8,128)(2,1)S(1)}, bf16[2,64,128]{2,1,0:T(8,128)(2,1)S(1)}, u32[]{:S(2)}, u32[]{:S(2)}) collective-permute-start(bf16[2,64,128]{2,1,0:T(8,128)(2,1)S(1)} %gather_fusion.8), channel_id=1, source_target_pairs={{0,32},{32,0},{8,40},{40,8},{16,48},{48,16},{24,56},{56,24},{64,96... | collective-permute-start | bytes 98312 | tf_op jit(solution)/shard_map/ppermute | solution.py:19
  50.0 3.6 %collective-permute-start.5 = (bf16[2,64,128]{2,1,0:T(8,128)(2,1)S(1)}, bf16[2,64,128]{2,1,0:T(8,128)(2,1)S(1)}, u32[]{:S(2)}, u32[]{:S(2)}) collective-permute-start(bf16[2,64,128]{2,1,0:T(8,128)(2,1)S(1)} %gather_fusion.7), channel_id=1, source_target_pairs={{0,16},{16,0},{8,24},{24,8},{32,48},{48,32},{40,56},{56,40},{64,80... | collective-permute-start | bytes 98312 | tf_op jit(solution)/shard_map/ppermute | solution.py:19
  53.6 2.8 %collective-permute-start.4 = (bf16[2,64,128]{2,1,0:T(8,128)(2,1)S(1)}, bf16[2,64,128]{2,1,0:T(8,128)(2,1)S(1)}, u32[]{:S(2)}, u32[]{:S(2)}) collective-permute-start(bf16[2,64,128]{2,1,0:T(8,128)(2,1)S(1)} %gather_fusion.6), channel_id=1, source_target_pairs={{0,8},{8,0},{16,24},{24,16},{32,40},{40,32},{48,56},{56,48},{64,72... | collective-permute-start | bytes 98312 | tf_op jit(solution)/shard_map/ppermute | solution.py:19
  56.4 2.2 %gather_fusion.5 = bf16[128,64,128]{2,1,0:T(8,128)(2,1)} fusion(bf16[32,64,128]{2,1,0:T(8,128)(2,1)S(1)} %get-tuple-element.42, s32[1024]{0:T(1024)S(1)} %pad_clamp_fusion.5), kind=kCustom, calls=%fused_computation.5 | custom fusion | bytes 4194816 | tf_op jit(solution)/shard_map/gather | solution.py:36
  58.8 0.7 fusion.47
  59.5 4.5 %fusion.121 = (bf16[32,64,128]{2,1,0:T(8,128)(2,1)S(1)}, f32[32,64,128]{2,1,0:T(8,128)}) fusion(f32[32,64,128]{2,1,0:T(8,128)} %get-tuple-element.43, f32[32,64,128]{2,0,1:T(8,128)S(1)} %fusion.47, bf16[32,4,64,64]{3,2,1,0:T(8,128)(2,1)S(1)} %copy-done, bf16[32,4,64,128]{3,2,1,0:T(8,128)(2,1)} %bitcast.201, ...), kind=kOutput, calls=%fused_computation.185 | convolution fusion | flops 136839168 | bytes 7872512 | tf_op jit(solution)/shard_map/rkab,rkbc->rac/dot_general | solution.py:37
  64.5 0.6 gather_fusion.13
  65.1 0.6 gather_fusion.12
  65.7 0.6 gather_fusion.11
  66.2 2.1 %collective-permute-start.11 = (bf16[2,64,128]{2,1,0:T(8,128)(2,1)S(1)}, bf16[2,64,128]{2,1,0:T(8,128)(2,1)S(1)}, u32[]{:S(2)}, u32[]{:S(2)}) collective-permute-start(bf16[2,64,128]{2,1,0:T(8,128)(2,1)S(1)} %gather_fusion.14), channel_id=1, source_target_pairs={{0,64},{64,0},{8,72},{72,8},{16,80},{80,16},{24,88},{88,24},{32,96... | collective-permute-start | bytes 98312 | tf_op jit(solution)/shard_map/ppermute | solution.py:19
  68.3 2.4 %collective-permute-start.10 = (bf16[2,64,128]{2,1,0:T(8,128)(2,1)S(1)}, bf16[2,64,128]{2,1,0:T(8,128)(2,1)S(1)}, u32[]{:S(2)}, u32[]{:S(2)}) collective-permute-start(bf16[2,64,128]{2,1,0:T(8,128)(2,1)S(1)} %gather_fusion.13), channel_id=1, source_target_pairs={{0,32},{32,0},{8,40},{40,8},{16,48},{48,16},{24,56},{56,24},{64,96... | collective-permute-start | bytes 98312 | tf_op jit(solution)/shard_map/ppermute | solution.py:19
  70.7 2.3 %collective-permute-start.9 = (bf16[2,64,128]{2,1,0:T(8,128)(2,1)S(1)}, bf16[2,64,128]{2,1,0:T(8,128)(2,1)S(1)}, u32[]{:S(2)}, u32[]{:S(2)}) collective-permute-start(bf16[2,64,128]{2,1,0:T(8,128)(2,1)S(1)} %gather_fusion.12), channel_id=1, source_target_pairs={{0,16},{16,0},{8,24},{24,8},{32,48},{48,32},{40,56},{56,40},{64,80... | collective-permute-start | bytes 98312 | tf_op jit(solution)/shard_map/ppermute | solution.py:19
  73.1 2.8 %collective-permute-start.8 = (bf16[2,64,128]{2,1,0:T(8,128)(2,1)S(1)}, bf16[2,64,128]{2,1,0:T(8,128)(2,1)S(1)}, u32[]{:S(2)}, u32[]{:S(2)}) collective-permute-start(bf16[2,64,128]{2,1,0:T(8,128)(2,1)S(1)} %gather_fusion.11), channel_id=1, source_target_pairs={{0,8},{8,0},{16,24},{24,16},{32,40},{40,32},{48,56},{56,48},{64,72... | collective-permute-start | bytes 98312 | tf_op jit(solution)/shard_map/ppermute | solution.py:19
  75.8 2.2 %gather_fusion.10 = bf16[128,64,128]{2,1,0:T(8,128)(2,1)} fusion(bf16[32,64,128]{2,1,0:T(8,128)(2,1)S(1)} %get-tuple-element.44, s32[1024]{0:T(1024)S(1)} %pad_clamp_fusion.5), kind=kCustom, calls=%fused_computation.10 | custom fusion | bytes 4194816 | tf_op jit(solution)/shard_map/gather | solution.py:36
  78.2 0.7 fusion.45
  78.9 4.5 %fusion.122 = (bf16[32,64,128]{2,1,0:T(8,128)(2,1)S(1)}, f32[32,64,128]{2,1,0:T(8,128)}) fusion(f32[32,64,128]{2,1,0:T(8,128)} %get-tuple-element.45, f32[32,64,128]{2,0,1:T(8,128)S(1)} %fusion.45, bf16[32,4,64,64]{3,2,1,0:T(8,128)(2,1)S(1)} %copy-done, bf16[32,4,64,128]{3,2,1,0:T(8,128)(2,1)} %bitcast.202, ...), kind=kOutput, calls=%fused_computation.186 | convolution fusion | flops 136839168 | bytes 7872512 | tf_op jit(solution)/shard_map/rkab,rkbc->rac/dot_general | solution.py:37
  84.0 0.6 gather_fusion.18
  84.5 0.6 gather_fusion.17
  85.1 0.6 gather_fusion.16
  85.7 5.9 %collective-permute-start.15 = (bf16[2,64,128]{2,1,0:T(8,128)(2,1)S(1)}, bf16[2,64,128]{2,1,0:T(8,128)(2,1)S(1)}, u32[]{:S(2)}, u32[]{:S(2)}) collective-permute-start(bf16[2,64,128]{2,1,0:T(8,128)(2,1)S(1)} %gather_fusion.19), channel_id=1, source_target_pairs={{0,64},{64,0},{8,72},{72,8},{16,80},{80,16},{24,88},{88,24},{32,96... | collective-permute-start | bytes 98312 | tf_op jit(solution)/shard_map/ppermute | solution.py:19
  91.5 4.3 %collective-permute-start.14 = (bf16[2,64,128]{2,1,0:T(8,128)(2,1)S(1)}, bf16[2,64,128]{2,1,0:T(8,128)(2,1)S(1)}, u32[]{:S(2)}, u32[]{:S(2)}) collective-permute-start(bf16[2,64,128]{2,1,0:T(8,128)(2,1)S(1)} %gather_fusion.18), channel_id=1, source_target_pairs={{0,32},{32,0},{8,40},{40,8},{16,48},{48,16},{24,56},{56,24},{64,96... | collective-permute-start | bytes 98312 | tf_op jit(solution)/shard_map/ppermute | solution.py:19
  95.9 3.6 %collective-permute-start.13 = (bf16[2,64,128]{2,1,0:T(8,128)(2,1)S(1)}, bf16[2,64,128]{2,1,0:T(8,128)(2,1)S(1)}, u32[]{:S(2)}, u32[]{:S(2)}) collective-permute-start(bf16[2,64,128]{2,1,0:T(8,128)(2,1)S(1)} %gather_fusion.17), channel_id=1, source_target_pairs={{0,16},{16,0},{8,24},{24,8},{32,48},{48,32},{40,56},{56,40},{64,80... | collective-permute-start | bytes 98312 | tf_op jit(solution)/shard_map/ppermute | solution.py:19
  99.5 2.9 %collective-permute-start.12 = (bf16[2,64,128]{2,1,0:T(8,128)(2,1)S(1)}, bf16[2,64,128]{2,1,0:T(8,128)(2,1)S(1)}, u32[]{:S(2)}, u32[]{:S(2)}) collective-permute-start(bf16[2,64,128]{2,1,0:T(8,128)(2,1)S(1)} %gather_fusion.16), channel_id=1, source_target_pairs={{0,8},{8,0},{16,24},{24,16},{32,40},{40,32},{48,56},{56,48},{64,72... | collective-permute-start | bytes 98312 | tf_op jit(solution)/shard_map/ppermute | solution.py:19
  102.5 2.2 %gather_fusion.15 = bf16[128,64,128]{2,1,0:T(8,128)(2,1)} fusion(bf16[32,64,128]{2,1,0:T(8,128)(2,1)S(1)} %get-tuple-element.46, s32[1024]{0:T(1024)S(1)} %pad_clamp_fusion.5), kind=kCustom, calls=%fused_computation.15 | custom fusion | bytes 4194816 | tf_op jit(solution)/shard_map/gather | solution.py:36
  104.8 0.7 fusion.43
  105.5 3.5 %fusion.26 = bf16[32,64,128]{2,1,0:T(8,128)(2,1)S(1)} fusion(f32[32,64,128]{2,1,0:T(8,128)} %get-tuple-element.47, bf16[32,4,64,64]{3,2,1,0:T(8,128)(2,1)S(1)} %copy-done, bf16[32,4,64,128]{3,2,1,0:T(8,128)(2,1)} %bitcast.204, bf16[32,64,128]{2,1,0:T(8,128)(2,1)} %param.20, f32[32,64,128]{2,0,1:T(8,128)S(1)} %fusion.43, ...), kind=kOutput, calls=%fused_computation.63 | convolution fusion | flops 136839168 | bytes 6823936 | tf_op jit(solution)/shard_map/rkab,rkbc->rac/dot_general | solution.py:37
  111.3 2.1 %collective-permute-start.19 = (bf16[2,64,128]{2,1,0:T(8,128)(2,1)S(1)}, bf16[2,64,128]{2,1,0:T(8,128)(2,1)S(1)}, u32[]{:S(2)}, u32[]{:S(2)}) collective-permute-start(bf16[2,64,128]{2,1,0:T(8,128)(2,1)S(1)} %gather_fusion.24), channel_id=1, source_target_pairs={{0,64},{64,0},{8,72},{72,8},{16,80},{80,16},{24,88},{88,24},{32,96... | collective-permute-start | bytes 98312 | tf_op jit(solution)/shard_map/ppermute | solution.py:19
  113.4 2.4 %collective-permute-start.18 = (bf16[2,64,128]{2,1,0:T(8,128)(2,1)S(1)}, bf16[2,64,128]{2,1,0:T(8,128)(2,1)S(1)}, u32[]{:S(2)}, u32[]{:S(2)}) collective-permute-start(bf16[2,64,128]{2,1,0:T(8,128)(2,1)S(1)} %gather_fusion.23), channel_id=1, source_target_pairs={{0,32},{32,0},{8,40},{40,8},{16,48},{48,16},{24,56},{56,24},{64,96... | collective-permute-start | bytes 98312 | tf_op jit(solution)/shard_map/ppermute | solution.py:19
  115.8 2.3 %collective-permute-start.17 = (bf16[2,64,128]{2,1,0:T(8,128)(2,1)S(1)}, bf16[2,64,128]{2,1,0:T(8,128)(2,1)S(1)}, u32[]{:S(2)}, u32[]{:S(2)}) collective-permute-start(bf16[2,64,128]{2,1,0:T(8,128)(2,1)S(1)} %gather_fusion.22), channel_id=1, source_target_pairs={{0,16},{16,0},{8,24},{24,8},{32,48},{48,32},{40,56},{56,40},{64,80... | collective-permute-start | bytes 98312 | tf_op jit(solution)/shard_map/ppermute | solution.py:19
  118.2 2.8 %collective-permute-start.16 = (bf16[2,64,128]{2,1,0:T(8,128)(2,1)S(1)}, bf16[2,64,128]{2,1,0:T(8,128)(2,1)S(1)}, u32[]{:S(2)}, u32[]{:S(2)}) collective-permute-start(bf16[2,64,128]{2,1,0:T(8,128)(2,1)S(1)} %gather_fusion.21), channel_id=1, source_target_pairs={{0,8},{8,0},{16,24},{24,16},{32,40},{40,32},{48,56},{56,48},{64,72... | collective-permute-start | bytes 98312 | tf_op jit(solution)/shard_map/ppermute | solution.py:19
  120.9 2.2 %gather_fusion.20 = bf16[128,64,128]{2,1,0:T(8,128)(2,1)} fusion(bf16[32,64,128]{2,1,0:T(8,128)(2,1)S(1)} %fusion.26, s32[1024]{0:T(1024)S(1)} %pad_clamp_fusion.5), kind=kCustom, calls=%fused_computation.20 | custom fusion | bytes 4194816 | tf_op jit(solution)/shard_map/gather | solution.py:36
  123.3 0.7 fusion.41
  124.0 3.9 %fusion.23 = bf16[32,64,128]{2,1,0:T(8,128)(2,1)} fusion(bf16[32,4,64,64]{3,2,1,0:T(8,128)(2,1)S(1)} %copy-done, bf16[32,4,64,128]{3,2,1,0:T(8,128)(2,1)} %bitcast.199, bf16[32,64,128]{2,1,0:T(8,128)(2,1)S(1)} %fusion.26, f32[32,64,128]{2,0,1:T(8,128)S(1)} %fusion.41, f32[32,64]{1,0:T(8,128)S(1)} %copy-done.3), kind=kOutput, calls=%fused_computation.60 | convolution fusion | flops 135790592 | bytes 5251072 | tf_op jit(solution)/shard_map/rkab,rkbc->rac/dot_general | solution.py:37
  128.7 4.0 %collective-permute-start.20 = (bf16[2,64,128]{2,0,1:T(2,128)(2,1)S(1)}, bf16[2,64,128]{2,0,1:T(2,128)(2,1)S(1)}, u32[]{:S(2)}, u32[]{:S(2)}) collective-permute-start(bf16[2,64,128]{2,0,1:T(2,128)(2,1)S(1)} %get-tuple-element.41), channel_id=1, source_target_pairs={{0,1},{1,2},{2,3},{3,4},{4,5},{5,6},{6,7},{8,9},{9,10},{10,11},{11... | collective-permute-start | bytes 98312 | tf_op jit(solution)/shard_map/ppermute | solution.py:29
  132.8 1.3 collective-permute-start.21
  134.6 2.0 gather_fusion.25
  136.6 1.3 dynamic-slice.18
  138.9 16.9 %all-reduce.2 = (s32[256]{0:T(256)S(1)}, s32[256]{0:T(256)S(1)}) all-reduce(s32[256]{0:T(256)S(1)} %dynamic-update-slice.6, s32[256]{0:T(256)S(1)} %bitcast_dynamic-update-slice_fusion), channel_id=1, replica_groups=mesh['elec'=64,'therm'=8] {'therm'}, use_global_device_ids=true, to_apply=%add | all-reduce | flops 512 | bytes 4096
  155.8 2.6 %convolution_bitcast_fusion = f32[32,128,64]{1,2,0:T(8,128)S(1)} fusion(bf16[32,3,64,64]{3,2,1,0:T(8,128)(2,1)} %param.30, bf16[32,3,64,128]{3,2,1,0:T(8,128)(2,1)} %bitcast.200), kind=kOutput, calls=%fused_computation.37 | convolution fusion | flops 100663296 | bytes 3407872 | tf_op jit(solution)/shard_map/rkab,rkbc->rac/dot_general | solution.py:37
  158.4 3.1 %bitcast_add_fusion = f32[32,64,128]{2,0,1:T(8,128)} fusion(f32[32,128,64]{1,2,0:T(8,128)S(1)} %convolution_bitcast_fusion, f32[32,64]{0,1:T(8,128)S(1)} %copy.82, bf16[32,64,128]{2,1,0:T(8,128)(2,1)S(1)} %copy-done.2, f32[32,64]{0,1:T(8,128)S(1)} %copy.83), kind=kLoop, calls=%fused_computation.80 | loop fusion | flops 2359296 | bytes 2637824 | tf_op jit(solution)/shard_map/add | solution.py:133
  161.9 1.7 fusion.87
  163.6 1.6 fusion.86
  165.2 22.6 %all-gather.3.cloned.1.call-done = bf16[256,64,128]{2,1,0:T(8,128)(2,1)} async-done(((bf16[32,64,128]{2,1,0:T(8,128)(2,1)}), bf16[256,64,128]{2,1,0:T(8,128)(2,1)}) %all-gather.3.cloned.1.call-update) | async-done | bytes 4194320 | tf_op jit(solution)/shard_map/all_gather | solution.py:114
  187.8 5.2 %convert_add_fusion = f32[32,64,128]{2,0,1:T(8,128)S(1)} fusion(f32[32,64,128]{2,0,1:T(8,128)} %fusion.86, bf16[256,64,128]{2,1,0:T(8,128)(2,1)} %all-gather.3.cloned.1.call-done, f32[32,64]{0,1:T(8,128)S(1)} %copy.91, bf16[32,64,128]{2,1,0:T(8,128)(2,1)S(1)} %copy-done.2, s32[256]{0:T(256)S(1)} %get-tuple-element.38, ...), kind=kOutput, calls=%fused_computation.33 | convolution fusion | flops 135544832 | bytes 6825216 | tf_op jit(solution)/shard_map/jr,rbc->jbc/dot_general | solution.py:120
  193.0 1.6 copy.92
  (90 shorter events, 7.2 us)
Async XLA Ops:
  7.2 26.1 %copy-start = (bf16[32,4,64,64]{3,2,1,0:T(8,128)(2,1)S(1)}, bf16[32,4,64,64]{3,2,1,0:T(8,128)(2,1)}, u32[]{:S(2)}) copy-start(bf16[32,4,64,64]{3,2,1,0:T(8,128)(2,1)} %param.22) | copy-start | bytes 3145732
  7.2 180.6 %all-gather.3.cloned.1.call-start = ((), (), s32[]{:S(2)}) async-start(), calls=%async_computation | async-start | bytes 4718592 | tf_op jit(solution)/shard_map/all_gather | solution.py:114
  10.3 22.1 %collective-permute-start.3 = (bf16[2,64,128]{2,1,0:T(8,128)(2,1)S(1)}, bf16[2,64,128]{2,1,0:T(8,128)(2,1)S(1)}, u32[]{:S(2)}, u32[]{:S(2)}) collective-permute-start(bf16[2,64,128]{2,1,0:T(8,128)(2,1)S(1)} %gather_fusion.4), channel_id=1, source_target_pairs={{0,64},{64,0},{8,72},{72,8},{16,80},{80,16},{24,88},{88,24},{32,96... | collective-permute-start | bytes 98312 | tf_op jit(solution)/shard_map/ppermute | solution.py:19
  19.2 13.3 %collective-permute-start.2 = (bf16[2,64,128]{2,1,0:T(8,128)(2,1)S(1)}, bf16[2,64,128]{2,1,0:T(8,128)(2,1)S(1)}, u32[]{:S(2)}, u32[]{:S(2)}) collective-permute-start(bf16[2,64,128]{2,1,0:T(8,128)(2,1)S(1)} %gather_fusion.3), channel_id=1, source_target_pairs={{0,32},{32,0},{8,40},{40,8},{16,48},{48,16},{24,56},{56,24},{64,96... | collective-permute-start | bytes 98312 | tf_op jit(solution)/shard_map/ppermute | solution.py:19
  22.2 10.2 %collective-permute-start.1 = (bf16[2,64,128]{2,1,0:T(8,128)(2,1)S(1)}, bf16[2,64,128]{2,1,0:T(8,128)(2,1)S(1)}, u32[]{:S(2)}, u32[]{:S(2)}) collective-permute-start(bf16[2,64,128]{2,1,0:T(8,128)(2,1)S(1)} %gather_fusion.2), channel_id=1, source_target_pairs={{0,16},{16,0},{8,24},{24,8},{32,48},{48,32},{40,56},{56,40},{64,80... | collective-permute-start | bytes 98312 | tf_op jit(solution)/shard_map/ppermute | solution.py:19
  25.1 7.4 %collective-permute-start = (bf16[2,64,128]{2,1,0:T(8,128)(2,1)S(1)}, bf16[2,64,128]{2,1,0:T(8,128)(2,1)S(1)}, u32[]{:S(2)}, u32[]{:S(2)}) collective-permute-start(bf16[2,64,128]{2,1,0:T(8,128)(2,1)S(1)} %gather_fusion.1), channel_id=1, source_target_pairs={{0,8},{8,0},{16,24},{24,16},{32,40},{40,32},{48,56},{56,48},{64,72... | collective-permute-start | bytes 98312 | tf_op jit(solution)/shard_map/ppermute | solution.py:19
  30.2 2.2 %copy-start.10 = (bf16[8,64,64]{2,1,0:T(8,128)(2,1)S(1)}, bf16[8,64,64]{2,1,0:T(8,128)(2,1)}, u32[]{:S(2)}) copy-start(bf16[8,64,64]{2,1,0:T(8,128)(2,1)} %param.25) | copy-start | bytes 196612
  30.2 3.1 %copy-start.3 = (f32[32,64]{1,0:T(8,128)S(1)}, f32[32,64]{1,0:T(8,128)}, u32[]{:S(2)}) copy-start(f32[32,64]{1,0:T(8,128)} %param.21) | copy-start | bytes 24580
  39.8 18.8 %collective-permute-start.7 = (bf16[2,64,128]{2,1,0:T(8,128)(2,1)S(1)}, bf16[2,64,128]{2,1,0:T(8,128)(2,1)S(1)}, u32[]{:S(2)}, u32[]{:S(2)}) collective-permute-start(bf16[2,64,128]{2,1,0:T(8,128)(2,1)S(1)} %gather_fusion.9), channel_id=1, source_target_pairs={{0,64},{64,0},{8,72},{72,8},{16,80},{80,16},{24,88},{88,24},{32,96... | collective-permute-start | bytes 98312 | tf_op jit(solution)/shard_map/ppermute | solution.py:19
  45.4 13.1 %collective-permute-start.6 = (bf16[2,64,128]{2,1,0:T(8,128)(2,1)S(1)}, bf16[2,64,128]{2,1,0:T(8,128)(2,1)S(1)}, u32[]{:S(2)}, u32[]{:S(2)}) collective-permute-start(bf16[2,64,128]{2,1,0:T(8,128)(2,1)S(1)} %gather_fusion.8), channel_id=1, source_target_pairs={{0,32},{32,0},{8,40},{40,8},{16,48},{48,16},{24,56},{56,24},{64,96... | collective-permute-start | bytes 98312 | tf_op jit(solution)/shard_map/ppermute | solution.py:19
  50.0 8.6 %collective-permute-start.5 = (bf16[2,64,128]{2,1,0:T(8,128)(2,1)S(1)}, bf16[2,64,128]{2,1,0:T(8,128)(2,1)S(1)}, u32[]{:S(2)}, u32[]{:S(2)}) collective-permute-start(bf16[2,64,128]{2,1,0:T(8,128)(2,1)S(1)} %gather_fusion.7), channel_id=1, source_target_pairs={{0,16},{16,0},{8,24},{24,8},{32,48},{48,32},{40,56},{56,40},{64,80... | collective-permute-start | bytes 98312 | tf_op jit(solution)/shard_map/ppermute | solution.py:19
  53.6 4.9 %collective-permute-start.4 = (bf16[2,64,128]{2,1,0:T(8,128)(2,1)S(1)}, bf16[2,64,128]{2,1,0:T(8,128)(2,1)S(1)}, u32[]{:S(2)}, u32[]{:S(2)}) collective-permute-start(bf16[2,64,128]{2,1,0:T(8,128)(2,1)S(1)} %gather_fusion.6), channel_id=1, source_target_pairs={{0,8},{8,0},{16,24},{24,16},{32,40},{40,32},{48,56},{56,48},{64,72... | collective-permute-start | bytes 98312 | tf_op jit(solution)/shard_map/ppermute | solution.py:19
  66.2 11.8 %collective-permute-start.11 = (bf16[2,64,128]{2,1,0:T(8,128)(2,1)S(1)}, bf16[2,64,128]{2,1,0:T(8,128)(2,1)S(1)}, u32[]{:S(2)}, u32[]{:S(2)}) collective-permute-start(bf16[2,64,128]{2,1,0:T(8,128)(2,1)S(1)} %gather_fusion.14), channel_id=1, source_target_pairs={{0,64},{64,0},{8,72},{72,8},{16,80},{80,16},{24,88},{88,24},{32,96... | collective-permute-start | bytes 98312 | tf_op jit(solution)/shard_map/ppermute | solution.py:19
  68.3 9.7 %collective-permute-start.10 = (bf16[2,64,128]{2,1,0:T(8,128)(2,1)S(1)}, bf16[2,64,128]{2,1,0:T(8,128)(2,1)S(1)}, u32[]{:S(2)}, u32[]{:S(2)}) collective-permute-start(bf16[2,64,128]{2,1,0:T(8,128)(2,1)S(1)} %gather_fusion.13), channel_id=1, source_target_pairs={{0,32},{32,0},{8,40},{40,8},{16,48},{48,16},{24,56},{56,24},{64,96... | collective-permute-start | bytes 98312 | tf_op jit(solution)/shard_map/ppermute | solution.py:19
  70.7 7.3 %collective-permute-start.9 = (bf16[2,64,128]{2,1,0:T(8,128)(2,1)S(1)}, bf16[2,64,128]{2,1,0:T(8,128)(2,1)S(1)}, u32[]{:S(2)}, u32[]{:S(2)}) collective-permute-start(bf16[2,64,128]{2,1,0:T(8,128)(2,1)S(1)} %gather_fusion.12), channel_id=1, source_target_pairs={{0,16},{16,0},{8,24},{24,8},{32,48},{48,32},{40,56},{56,40},{64,80... | collective-permute-start | bytes 98312 | tf_op jit(solution)/shard_map/ppermute | solution.py:19
  73.1 4.9 %collective-permute-start.8 = (bf16[2,64,128]{2,1,0:T(8,128)(2,1)S(1)}, bf16[2,64,128]{2,1,0:T(8,128)(2,1)S(1)}, u32[]{:S(2)}, u32[]{:S(2)}) collective-permute-start(bf16[2,64,128]{2,1,0:T(8,128)(2,1)S(1)} %gather_fusion.11), channel_id=1, source_target_pairs={{0,8},{8,0},{16,24},{24,16},{32,40},{40,32},{48,56},{56,48},{64,72... | collective-permute-start | bytes 98312 | tf_op jit(solution)/shard_map/ppermute | solution.py:19
  85.7 19.0 %collective-permute-start.15 = (bf16[2,64,128]{2,1,0:T(8,128)(2,1)S(1)}, bf16[2,64,128]{2,1,0:T(8,128)(2,1)S(1)}, u32[]{:S(2)}, u32[]{:S(2)}) collective-permute-start(bf16[2,64,128]{2,1,0:T(8,128)(2,1)S(1)} %gather_fusion.19), channel_id=1, source_target_pairs={{0,64},{64,0},{8,72},{72,8},{16,80},{80,16},{24,88},{88,24},{32,96... | collective-permute-start | bytes 98312 | tf_op jit(solution)/shard_map/ppermute | solution.py:19
  91.5 13.1 %collective-permute-start.14 = (bf16[2,64,128]{2,1,0:T(8,128)(2,1)S(1)}, bf16[2,64,128]{2,1,0:T(8,128)(2,1)S(1)}, u32[]{:S(2)}, u32[]{:S(2)}) collective-permute-start(bf16[2,64,128]{2,1,0:T(8,128)(2,1)S(1)} %gather_fusion.18), channel_id=1, source_target_pairs={{0,32},{32,0},{8,40},{40,8},{16,48},{48,16},{24,56},{56,24},{64,96... | collective-permute-start | bytes 98312 | tf_op jit(solution)/shard_map/ppermute | solution.py:19
  95.9 8.8 %collective-permute-start.13 = (bf16[2,64,128]{2,1,0:T(8,128)(2,1)S(1)}, bf16[2,64,128]{2,1,0:T(8,128)(2,1)S(1)}, u32[]{:S(2)}, u32[]{:S(2)}) collective-permute-start(bf16[2,64,128]{2,1,0:T(8,128)(2,1)S(1)} %gather_fusion.17), channel_id=1, source_target_pairs={{0,16},{16,0},{8,24},{24,8},{32,48},{48,32},{40,56},{56,40},{64,80... | collective-permute-start | bytes 98312 | tf_op jit(solution)/shard_map/ppermute | solution.py:19
  99.5 5.1 %collective-permute-start.12 = (bf16[2,64,128]{2,1,0:T(8,128)(2,1)S(1)}, bf16[2,64,128]{2,1,0:T(8,128)(2,1)S(1)}, u32[]{:S(2)}, u32[]{:S(2)}) collective-permute-start(bf16[2,64,128]{2,1,0:T(8,128)(2,1)S(1)} %gather_fusion.16), channel_id=1, source_target_pairs={{0,8},{8,0},{16,24},{24,16},{32,40},{40,32},{48,56},{56,48},{64,72... | collective-permute-start | bytes 98312 | tf_op jit(solution)/shard_map/ppermute | solution.py:19
  109.1 14.9 %copy-start.1 = (bf16[32,64,128]{2,1,0:T(8,128)(2,1)}, bf16[32,64,128]{2,1,0:T(8,128)(2,1)S(1)}, u32[]{:S(2)}) copy-start(bf16[32,64,128]{2,1,0:T(8,128)(2,1)S(1)} %fusion.26) | copy-start | bytes 1572868
  111.3 11.8 %collective-permute-start.19 = (bf16[2,64,128]{2,1,0:T(8,128)(2,1)S(1)}, bf16[2,64,128]{2,1,0:T(8,128)(2,1)S(1)}, u32[]{:S(2)}, u32[]{:S(2)}) collective-permute-start(bf16[2,64,128]{2,1,0:T(8,128)(2,1)S(1)} %gather_fusion.24), channel_id=1, source_target_pairs={{0,64},{64,0},{8,72},{72,8},{16,80},{80,16},{24,88},{88,24},{32,96... | collective-permute-start | bytes 98312 | tf_op jit(solution)/shard_map/ppermute | solution.py:19
  113.4 9.7 %collective-permute-start.18 = (bf16[2,64,128]{2,1,0:T(8,128)(2,1)S(1)}, bf16[2,64,128]{2,1,0:T(8,128)(2,1)S(1)}, u32[]{:S(2)}, u32[]{:S(2)}) collective-permute-start(bf16[2,64,128]{2,1,0:T(8,128)(2,1)S(1)} %gather_fusion.23), channel_id=1, source_target_pairs={{0,32},{32,0},{8,40},{40,8},{16,48},{48,16},{24,56},{56,24},{64,96... | collective-permute-start | bytes 98312 | tf_op jit(solution)/shard_map/ppermute | solution.py:19
  115.8 7.2 %collective-permute-start.17 = (bf16[2,64,128]{2,1,0:T(8,128)(2,1)S(1)}, bf16[2,64,128]{2,1,0:T(8,128)(2,1)S(1)}, u32[]{:S(2)}, u32[]{:S(2)}) collective-permute-start(bf16[2,64,128]{2,1,0:T(8,128)(2,1)S(1)} %gather_fusion.22), channel_id=1, source_target_pairs={{0,16},{16,0},{8,24},{24,8},{32,48},{48,32},{40,56},{56,40},{64,80... | collective-permute-start | bytes 98312 | tf_op jit(solution)/shard_map/ppermute | solution.py:19
  118.2 4.9 %collective-permute-start.16 = (bf16[2,64,128]{2,1,0:T(8,128)(2,1)S(1)}, bf16[2,64,128]{2,1,0:T(8,128)(2,1)S(1)}, u32[]{:S(2)}, u32[]{:S(2)}) collective-permute-start(bf16[2,64,128]{2,1,0:T(8,128)(2,1)S(1)} %gather_fusion.21), channel_id=1, source_target_pairs={{0,8},{8,0},{16,24},{24,16},{32,40},{40,32},{48,56},{56,48},{64,72... | collective-permute-start | bytes 98312 | tf_op jit(solution)/shard_map/ppermute | solution.py:19
  124.0 4.0 %copy-start.7 = (s32[32,64]{1,0:T(8,128)S(1)}, s32[32,64]{1,0:T(8,128)}, u32[]{:S(2)}) copy-start(s32[32,64]{1,0:T(8,128)} %param.33) | copy-start | bytes 24580
  124.0 4.0 %copy-start.9 = (f32[8]{0:T(128)S(1)}, f32[8]{0:T(128)}, u32[]{:S(2)}) copy-start(f32[8]{0:T(128)} %param.34) | copy-start | bytes 100
  124.0 4.2 %copy-start.2 = (bf16[32,64,128]{2,1,0:T(8,128)(2,1)S(1)}, bf16[32,64,128]{2,1,0:T(8,128)(2,1)}, u32[]{:S(2)}) copy-start(bf16[32,64,128]{2,1,0:T(8,128)(2,1)} %param.28) | copy-start | bytes 1572868
  127.9 6.4 %copy-start.8 = (s32[32,3]{0,1:T(4,128)S(1)}, s32[32,3]{0,1:T(4,128)}, u32[]{:S(2)}) copy-start(s32[32,3]{0,1:T(4,128)} %param.31) | copy-start | bytes 1156
  127.9 6.6 %copy-start.5 = (f32[32,64]{1,0:T(8,128)S(1)}, f32[32,64]{1,0:T(8,128)}, u32[]{:S(2)}) copy-start(f32[32,64]{1,0:T(8,128)} %param.29) | copy-start | bytes 24580
  128.7 32.9 %collective-permute-start.20 = (bf16[2,64,128]{2,0,1:T(2,128)(2,1)S(1)}, bf16[2,64,128]{2,0,1:T(2,128)(2,1)S(1)}, u32[]{:S(2)}, u32[]{:S(2)}) collective-permute-start(bf16[2,64,128]{2,0,1:T(2,128)(2,1)S(1)} %get-tuple-element.41), channel_id=1, source_target_pairs={{0,1},{1,2},{2,3},{3,4},{4,5},{5,6},{6,7},{8,9},{9,10},{10,11},{11... | collective-permute-start | bytes 98312 | tf_op jit(solution)/shard_map/ppermute | solution.py:29
  132.7 5.8 %copy-start.11 = (s32[32]{0:T(128)S(1)}, s32[32]{0:T(128)}, u32[]{:S(2)}) copy-start(s32[32]{0:T(128)} %param.27) | copy-start | bytes 388
  132.8 6.0 %copy-start.12 = (s32[32,1]{0,1:T(1,128)S(1)}, s32[32,1]{0,1:T(1,128)}, u32[]{:S(2)}) copy-start(s32[32,1]{0,1:T(1,128)} %param.26) | copy-start | bytes 388
  132.8 29.0 %collective-permute-start.21 = (bf16[2,64,128]{2,0,1:T(2,128)(2,1)S(1)}, bf16[2,64,128]{2,0,1:T(2,128)(2,1)S(1)}, u32[]{:S(2)}, u32[]{:S(2)}) collective-permute-start(bf16[2,64,128]{2,0,1:T(2,128)(2,1)S(1)} %get-tuple-element.40), channel_id=1, source_target_pairs={{1,0},{2,1},{3,2},{4,3},{5,4},{6,5},{7,6},{9,8},{10,9},{11,10},{12... | collective-permute-start | bytes 98312 | tf_op jit(solution)/shard_map/ppermute | solution.py:30
  158.4 3.2 %copy-start.6 = (f32[32,64]{1,0:T(8,128)S(1)}, f32[32,64]{1,0:T(8,128)}, u32[]{:S(2)}) copy-start(f32[32,64]{1,0:T(8,128)} %param.35) | copy-start | bytes 24580
  158.4 3.2 %copy-start.4 = (bf16[4,64,64]{2,1,0:T(8,128)(2,1)S(1)}, bf16[4,64,64]{2,1,0:T(8,128)(2,1)}, u32[]{:S(2)}) copy-start(bf16[4,64,64]{2,1,0:T(8,128)(2,1)} %param.32) | copy-start | bytes 98308
Sparse Core Ops, SparseCore 0:
  128.1 59.6 all-gather.2
where the time goes:
time: 202 us; the launch traced here: 201 us
  starting transfers between devices  74.3 us (37%)
  matrix products  33 us (16%)
  local copies, waits for them, and re-layouts  30 us (15%)
  waiting for transfers between devices  22.6 us (11%)
  blocking collectives  16.9 us (8%)
  between operations  15.3 us (8%)
  other arithmetic  9.17 us (5%)
    ppermute x20, starting transfers between devices, from_partner(): return lax.ppermute(block, axis, route)  68.9 us
    dot_general x6, matrix products, near_product(): jnp.einsum('rkab,rkbc->rac', near_blocks, picked, preferred_element_type=...  23.3 us
    all_gather x1, waiting for transfers between devices, body(): heat_piece = lax.all_gather(heat_b, 'therm', axis=0, tiled=True)  22.6 us
    unnamed x1, blocking collectives  16.9 us
    gather x6, local copies, waits for them, and re-layouts, near_product(): picked = field_b[near_index]  12.8 us
    gather x20, local copies, waits for them, and re-layouts, electric_apply(): outgoing = field_b[interface_tiles_per_level[level_bit]]  11.2 us
    dot_general x1, matrix products, body(): jnp.einsum('jr,rbc->jbc', selector, heat_piece, preferred_element_type=jn...  5.19 us
    unnamed x35, local copies, waits for them, and re-layouts  4.18 us
  transfers between devices with their start and end apart: 23, of which 1 were waited for; matrix products, arithmetic and copies ran while one was open for 14% of the time, Pallas kernels for 0%

commit v1 on v0

--- a/solution.py
+++ b/solution.py
@@ -111,7 +111,23 @@
     warmth_tile_count = warmth_values.shape[0]
     block_ids = jnp.arange(warmth_tile_count)[:, None]
     own_index = lax.axis_index("therm")
-    heat_piece = lax.all_gather(heat_b, "therm", axis=0, tiled=True)
+    ways, here, turn = (lax.axis_size("therm"), lax.axis_index("therm"), heat_b.shape[0])
+    lengths = [n * ways if d == 0 else n for d, n in enumerate(heat_b.shape)]
+    full = lax.dynamic_update_slice_in_dim(
+        jnp.zeros(lengths, heat_b.dtype), heat_b, here * turn, axis=0
+    )
+    going_up = going_down = heat_b
+    for far in range(1, ways // 2 + 1):
+        going_up = lax.ppermute(going_up, "therm", [(d, (d + 1) % ways) for d in range(ways)])
+        full = lax.dynamic_update_slice_in_dim(full, going_up, (here - far) % ways * turn, axis=0)
+        if 2 * far < ways:
+            going_down = lax.ppermute(
+                going_down, "therm", [(d, (d - 1) % ways) for d in range(ways)]
+            )
+            full = lax.dynamic_update_slice_in_dim(
+                full, going_down, (here + far) % ways * turn, axis=0
+            )
+    heat_piece = full
     owner_piece = lax.all_gather(owners, "therm", axis=0, tiled=True)
     row_piece = lax.all_gather(warmth_receiver_tile, "therm", axis=0, tiled=True)
     selector = ((row_piece[None, :] == block_ids) & (owner_piece[None, :] == own_index)).astype(

time: 202 us -> 217 us (1.074)
  the two profiles are of different devices: /device:TPU:1 before, /device:TPU:6 now
where the time goes in v1:
time: 217 us; the launch traced here: 215 us
  starting transfers between devices  93.3 us (43%)
  local copies, waits for them, and re-layouts  35.3 us (16%)
  matrix products  31.5 us (15%)
  waiting for transfers between devices  23.9 us (11%)
  blocking collectives  18 us (8%)
  other arithmetic  11 us (5%)
  between operations  2.33 us (1%)
    ppermute x20, starting transfers between devices, from_partner(): return lax.ppermute(block, axis, route)  64.8 us
    dot_general x6, matrix products, near_product(): jnp.einsum('rkab,rkbc->rac', near_blocks, picked, preferred_element_type=...  23.6 us
    ppermute x4, waiting for transfers between devices, body(): lax.ppermute(going_up, 'therm', [(d, (d + 1) % ways) for d in range(ways)])  20.1 us
    unnamed x1, blocking collectives  18 us
    gather x6, local copies, waits for them, and re-layouts, near_product(): picked = field_b[near_index]  12.8 us
    ppermute x4, starting transfers between devices, body(): lax.ppermute(going_up, 'therm', [(d, (d + 1) % ways) for d in range(ways)])  11.6 us
    ppermute x3, starting transfers between devices, body(): lax.ppermute(going_down, 'therm', [(d, (d - 1) % ways) for d in range(way...  11.3 us
    gather x20, local copies, waits for them, and re-layouts, electric_apply(): outgoing = field_b[interface_tiles_per_level[level_bit]]  11.2 us
  transfers between devices with their start and end apart: 29, of which 6 were waited for; matrix products, arithmetic and copies ran while one was open for 33% of the time, Pallas kernels for 0%

profile of v1, /device:TPU:6, one launch (start us, length us, event | category | flops | bytes accessed | tf_op | source)
XLA Modules:
  0.0 215.3 jit_solution(5975762769222326754)
XLA Ops:
  0.7 1.1 slice_reduce_fusion.3
  1.8 1.4 fusion.32
  3.7 1.9 collective-permute-start
  6.2 3.5 %collective-permute-start.1 = (bf16[2,64,128]{2,1,0:T(8,128)(2,1)S(1)}, bf16[2,64,128]{2,1,0:T(8,128)(2,1)S(1)}, u32[]{:S(2)}, u32[]{:S(2)}) collective-permute-start(bf16[2,64,128]{2,1,0:T(8,128)(2,1)S(1)} %gather_fusion.2), channel_id=1, source_target_pairs={{0,16},{16,0},{8,24},{24,8},{32,48},{48,32},{40,56},{56,40},{64,80... | collective-permute-start | bytes 98312 | tf_op jit(solution)/shard_map/ppermute | solution.py:19
  10.3 4.5 %collective-permute-start.2 = (bf16[2,64,128]{2,1,0:T(8,128)(2,1)S(1)}, bf16[2,64,128]{2,1,0:T(8,128)(2,1)}, u32[]{:S(2)}, u32[]{:S(2)}) collective-permute-start(bf16[2,64,128]{2,1,0:T(8,128)(2,1)S(1)} %gather_fusion.3), channel_id=1, source_target_pairs={{0,32},{32,0},{8,40},{40,8},{16,48},{48,16},{24,56},{56,24},{64,96... | collective-permute-start | bytes 98312 | tf_op jit(solution)/shard_map/ppermute | solution.py:19
  15.4 5.0 %collective-permute-start.3 = (bf16[2,64,128]{2,1,0:T(8,128)(2,1)S(1)}, bf16[2,64,128]{2,1,0:T(8,128)(2,1)}, u32[]{:S(2)}, u32[]{:S(2)}) collective-permute-start(bf16[2,64,128]{2,1,0:T(8,128)(2,1)S(1)} %gather_fusion.4), channel_id=1, source_target_pairs={{0,64},{64,0},{8,72},{72,8},{16,80},{80,16},{24,88},{88,24},{32,96... | collective-permute-start | bytes 98312 | tf_op jit(solution)/shard_map/ppermute | solution.py:19
  20.5 0.8 select_reduce_fusion
  21.4 1.5 fusion.30
  22.9 0.8 copy-done.3
  23.8 4.3 %collective-permute-start.27 = (bf16[2,64,128]{2,0,1:T(2,128)(2,1)S(1)}, bf16[2,64,128]{2,0,1:T(2,128)(2,1)S(1)}, u32[]{:S(2)}, u32[]{:S(2)}) collective-permute-start(bf16[2,64,128]{2,0,1:T(2,128)(2,1)S(1)} %get-tuple-element.39), channel_id=1, source_target_pairs={{0,1},{1,2},{2,3},{3,4},{4,5},{5,6},{6,7},{8,9},{9,10},{10,11},{11... | collective-permute-start | bytes 98312 | tf_op jit(solution)/shard_map/ppermute | solution.py:29
  28.5 2.2 %gather_fusion = bf16[128,64,128]{2,1,0:T(8,128)(2,1)} fusion(bf16[32,64,128]{2,1,0:T(8,128)(2,1)S(1)} %fusion.32, s32[1024]{0:T(1024)S(1)} %pad_clamp_fusion.5), kind=kCustom, calls=%fused_computation | custom fusion | bytes 4194816 | tf_op jit(solution)/shard_map/gather | solution.py:36
  30.9 1.1 convolution_bitcast_fusion.10
  32.7 4.1 %fusion.112 = (bf16[32,64,128]{2,1,0:T(8,128)(2,1)S(1)}, f32[32,64,128]{2,1,0:T(8,128)}) fusion(f32[32,64,128]{2,0,1:T(8,128)S(1)} %fusion.41, bf16[32,4,64,64]{3,2,1,0:T(8,128)(2,1)S(1)} %copy-done, bf16[32,4,64,128]{3,2,1,0:T(8,128)(2,1)} %bitcast.202, f32[32,64]{1,0:T(8,128)S(1)} %copy-done.8, bf16[32,64,128]{2,1,0:T(8,128)(2,1)S(1)} %copy-done.7), kind=kOutput, calls=%fused_computation.191 | convolution fusion | flops 137625600 | bytes 6299648 | tf_op jit(solution)/shard_map/rkab,rkbc->rac/dot_general | solution.py:37
  39.1 1.9 collective-permute-start.4
  41.0 3.3 %collective-permute-start.5 = (bf16[2,64,128]{2,1,0:T(8,128)(2,1)S(1)}, bf16[2,64,128]{2,1,0:T(8,128)(2,1)S(1)}, u32[]{:S(2)}, u32[]{:S(2)}) collective-permute-start(bf16[2,64,128]{2,1,0:T(8,128)(2,1)S(1)} %gather_fusion.7), channel_id=1, source_target_pairs={{0,16},{16,0},{8,24},{24,8},{32,48},{48,32},{40,56},{56,40},{64,80... | collective-permute-start | bytes 98312 | tf_op jit(solution)/shard_map/ppermute | solution.py:19
  44.3 4.0 %collective-permute-start.6 = (bf16[2,64,128]{2,1,0:T(8,128)(2,1)S(1)}, bf16[2,64,128]{2,1,0:T(8,128)(2,1)}, u32[]{:S(2)}, u32[]{:S(2)}) collective-permute-start(bf16[2,64,128]{2,1,0:T(8,128)(2,1)S(1)} %gather_fusion.8), channel_id=1, source_target_pairs={{0,32},{32,0},{8,40},{40,8},{16,48},{48,16},{24,56},{56,24},{64,96... | collective-permute-start | bytes 98312 | tf_op jit(solution)/shard_map/ppermute | solution.py:19
  48.3 2.0 collective-permute-start.7
  50.4 1.2 copy.89
  51.6 1.9 gather_fusion.25
  53.6 2.2 %gather_fusion.5 = bf16[128,64,128]{2,1,0:T(8,128)(2,1)} fusion(bf16[32,64,128]{2,1,0:T(8,128)(2,1)S(1)} %get-tuple-element.40, s32[1024]{0:T(1024)S(1)} %pad_clamp_fusion.5), kind=kCustom, calls=%fused_computation.5 | custom fusion | bytes 4194816 | tf_op jit(solution)/shard_map/gather | solution.py:36
  55.8 2.7 %collective-permute-done.7 = bf16[2,64,128]{2,1,0:T(8,128)(2,1)} collective-permute-done((bf16[2,64,128]{2,1,0:T(8,128)(2,1)S(1)}, bf16[2,64,128]{2,1,0:T(8,128)(2,1)}, u32[]{:S(2)}, u32[]{:S(2)}) %collective-permute-start.7) | collective-permute-done | bytes 32800 | tf_op jit(solution)/shard_map/ppermute | solution.py:19
  58.4 0.9 convolution_bitcast_fusion.9
  60.1 4.5 %fusion.113 = (bf16[32,64,128]{2,1,0:T(8,128)(2,1)S(1)}, f32[32,64,128]{2,1,0:T(8,128)}) fusion(f32[32,64,128]{2,1,0:T(8,128)} %get-tuple-element.41, f32[32,64,128]{2,0,1:T(8,128)S(1)} %fusion.39, bf16[32,4,64,64]{3,2,1,0:T(8,128)(2,1)S(1)} %copy-done, bf16[32,4,64,128]{3,2,1,0:T(8,128)(2,1)} %bitcast.203, ...), kind=kOutput, calls=%fused_computation.192 | convolution fusion | flops 136839168 | bytes 7872512 | tf_op jit(solution)/shard_map/rkab,rkbc->rac/dot_general | solution.py:37
  66.8 2.4 %collective-permute-start.10 = (bf16[2,64,128]{2,1,0:T(8,128)(2,1)S(1)}, bf16[2,64,128]{2,1,0:T(8,128)(2,1)S(1)}, u32[]{:S(2)}, u32[]{:S(2)}) collective-permute-start(bf16[2,64,128]{2,1,0:T(8,128)(2,1)S(1)} %gather_fusion.13), channel_id=1, source_target_pairs={{0,32},{32,0},{8,40},{40,8},{16,48},{48,16},{24,56},{56,24},{64,96... | collective-permute-start | bytes 98312 | tf_op jit(solution)/shard_map/ppermute | solution.py:19
  69.3 1.9 collective-permute-start.8
  71.2 2.9 %collective-permute-start.9 = (bf16[2,64,128]{2,1,0:T(8,128)(2,1)S(1)}, bf16[2,64,128]{2,1,0:T(8,128)(2,1)S(1)}, u32[]{:S(2)}, u32[]{:S(2)}) collective-permute-start(bf16[2,64,128]{2,1,0:T(8,128)(2,1)S(1)} %gather_fusion.12), channel_id=1, source_target_pairs={{0,16},{16,0},{8,24},{24,8},{32,48},{48,32},{40,56},{56,40},{64,80... | collective-permute-start | bytes 98312 | tf_op jit(solution)/shard_map/ppermute | solution.py:19
  74.2 5.0 %collective-permute-start.11 = (bf16[2,64,128]{2,1,0:T(8,128)(2,1)S(1)}, bf16[2,64,128]{2,1,0:T(8,128)(2,1)S(1)}, u32[]{:S(2)}, u32[]{:S(2)}) collective-permute-start(bf16[2,64,128]{2,1,0:T(8,128)(2,1)S(1)} %gather_fusion.14), channel_id=1, source_target_pairs={{0,64},{64,0},{8,72},{72,8},{16,80},{80,16},{24,88},{88,24},{32,96... | collective-permute-start | bytes 98312 | tf_op jit(solution)/shard_map/ppermute | solution.py:19
  79.2 3.6 %convolution_bitcast_fusion = f32[32,128,64]{1,2,0:T(8,128)} fusion(bf16[32,3,64,64]{3,2,1,0:T(8,128)(2,1)} %param.30, bf16[32,3,64,128]{3,2,1,0:T(8,128)(2,1)} %bitcast.201), kind=kOutput, calls=%fused_computation.34 | convolution fusion | flops 100663296 | bytes 3407872 | tf_op jit(solution)/shard_map/rkab,rkbc->rac/dot_general | solution.py:37
  82.9 2.2 %gather_fusion.10 = bf16[128,64,128]{2,1,0:T(8,128)(2,1)} fusion(bf16[32,64,128]{2,1,0:T(8,128)(2,1)S(1)} %get-tuple-element.42, s32[1024]{0:T(1024)S(1)} %pad_clamp_fusion.5), kind=kCustom, calls=%fused_computation.10 | custom fusion | bytes 4194816 | tf_op jit(solution)/shard_map/gather | solution.py:36
  85.9 4.7 %fusion.114 = (bf16[32,64,128]{2,1,0:T(8,128)(2,1)S(1)}, f32[32,64,128]{2,1,0:T(8,128)}) fusion(f32[32,64,128]{2,1,0:T(8,128)} %get-tuple-element.43, f32[32,64,128]{2,0,1:T(8,128)S(1)} %fusion.37, bf16[32,4,64,64]{3,2,1,0:T(8,128)(2,1)S(1)} %copy-done, bf16[32,4,64,128]{3,2,1,0:T(8,128)(2,1)} %bitcast.204, bf16[32,64,128]{2,1,0:T(8,128)(2,1)} %copy-done.2, ...), kind=kOutput, calls=%fused_computation.193 | convolution fusion | flops 136839168 | bytes 7872512 | tf_op jit(solution)/shard_map/rkab,rkbc->rac/dot_general | solution.py:37
  92.9 1.9 collective-permute-start.12
  94.8 3.2 %collective-permute-start.13 = (bf16[2,64,128]{2,1,0:T(8,128)(2,1)S(1)}, bf16[2,64,128]{2,1,0:T(8,128)(2,1)S(1)}, u32[]{:S(2)}, u32[]{:S(2)}) collective-permute-start(bf16[2,64,128]{2,1,0:T(8,128)(2,1)S(1)} %gather_fusion.17), channel_id=1, source_target_pairs={{0,16},{16,0},{8,24},{24,8},{32,48},{48,32},{40,56},{56,40},{64,80... | collective-permute-start | bytes 98312 | tf_op jit(solution)/shard_map/ppermute | solution.py:19
  98.1 4.1 %collective-permute-start.14 = (bf16[2,64,128]{2,1,0:T(8,128)(2,1)S(1)}, bf16[2,64,128]{2,1,0:T(8,128)(2,1)}, u32[]{:S(2)}, u32[]{:S(2)}) collective-permute-start(bf16[2,64,128]{2,1,0:T(8,128)(2,1)S(1)} %gather_fusion.18), channel_id=1, source_target_pairs={{0,32},{32,0},{8,40},{40,8},{16,48},{48,16},{24,56},{56,24},{64,96... | collective-permute-start | bytes 98312 | tf_op jit(solution)/shard_map/ppermute | solution.py:19
  102.2 4.8 %collective-permute-start.15 = (bf16[2,64,128]{2,1,0:T(8,128)(2,1)S(1)}, bf16[2,64,128]{2,1,0:T(8,128)(2,1)}, u32[]{:S(2)}, u32[]{:S(2)}) collective-permute-start(bf16[2,64,128]{2,1,0:T(8,128)(2,1)S(1)} %gather_fusion.19), channel_id=1, source_target_pairs={{0,64},{64,0},{8,72},{72,8},{16,80},{80,16},{24,88},{88,24},{32,96... | collective-permute-start | bytes 98312 | tf_op jit(solution)/shard_map/ppermute | solution.py:19
  107.0 3.9 %bitcast_add_fusion = f32[32,64,128]{2,0,1:T(8,128)} fusion(f32[32,128,64]{1,2,0:T(8,128)} %convolution_bitcast_fusion, f32[32,64]{0,1:T(8,128)S(1)} %copy.86, bf16[32,64,128]{2,1,0:T(8,128)(2,1)S(1)} %copy-done.4, f32[32,64]{0,1:T(8,128)S(1)} %copy.87), kind=kLoop, calls=%fused_computation.79 | loop fusion | flops 2359296 | bytes 2637824 | tf_op jit(solution)/shard_map/add | solution.py:149
  110.9 1.3 dynamic-slice.18
  112.8 2.2 %gather_fusion.15 = bf16[128,64,128]{2,1,0:T(8,128)(2,1)} fusion(bf16[32,64,128]{2,1,0:T(8,128)(2,1)S(1)} %get-tuple-element.44, s32[1024]{0:T(1024)S(1)} %pad_clamp_fusion.5), kind=kCustom, calls=%fused_computation.15 | custom fusion | bytes 4194816 | tf_op jit(solution)/shard_map/gather | solution.py:36
  115.0 0.9 convolution_bitcast_fusion.7
  116.7 3.6 %fusion.20 = bf16[32,64,128]{2,1,0:T(8,128)(2,1)S(1)} fusion(f32[32,64,128]{2,1,0:T(8,128)} %get-tuple-element.45, bf16[32,4,64,64]{3,2,1,0:T(8,128)(2,1)S(1)} %copy-done, bf16[32,4,64,128]{3,2,1,0:T(8,128)(2,1)} %bitcast.205, bf16[32,64,128]{2,1,0:T(8,128)(2,1)} %param.20, f32[32,64,128]{2,0,1:T(8,128)S(1)} %fusion.35, ...), kind=kOutput, calls=%fused_computation.62 | convolution fusion | flops 136839168 | bytes 6823936 | tf_op jit(solution)/shard_map/rkab,rkbc->rac/dot_general | solution.py:37
  122.5 1.9 collective-permute-start.16
  124.4 2.7 %collective-permute-start.17 = (bf16[2,64,128]{2,1,0:T(8,128)(2,1)S(1)}, bf16[2,64,128]{2,1,0:T(8,128)(2,1)S(1)}, u32[]{:S(2)}, u32[]{:S(2)}) collective-permute-start(bf16[2,64,128]{2,1,0:T(8,128)(2,1)S(1)} %gather_fusion.22), channel_id=1, source_target_pairs={{0,16},{16,0},{8,24},{24,8},{32,48},{48,32},{40,56},{56,40},{64,80... | collective-permute-start | bytes 98312 | tf_op jit(solution)/shard_map/ppermute | solution.py:19
  127.1 2.7 %collective-permute-start.18 = (bf16[2,64,128]{2,1,0:T(8,128)(2,1)S(1)}, bf16[2,64,128]{2,1,0:T(8,128)(2,1)S(1)}, u32[]{:S(2)}, u32[]{:S(2)}) collective-permute-start(bf16[2,64,128]{2,1,0:T(8,128)(2,1)S(1)} %gather_fusion.23), channel_id=1, source_target_pairs={{0,32},{32,0},{8,40},{40,8},{16,48},{48,16},{24,56},{56,24},{64,96... | collective-permute-start | bytes 98312 | tf_op jit(solution)/shard_map/ppermute | solution.py:19
  129.8 5.0 %collective-permute-start.19 = (bf16[2,64,128]{2,1,0:T(8,128)(2,1)S(1)}, bf16[2,64,128]{2,1,0:T(8,128)(2,1)S(1)}, u32[]{:S(2)}, u32[]{:S(2)}) collective-permute-start(bf16[2,64,128]{2,1,0:T(8,128)(2,1)S(1)} %gather_fusion.24), channel_id=1, source_target_pairs={{0,64},{64,0},{8,72},{72,8},{16,80},{80,16},{24,88},{88,24},{32,96... | collective-permute-start | bytes 98312 | tf_op jit(solution)/shard_map/ppermute | solution.py:19
  135.2 18.0 %all-reduce.2 = (s32[256]{0:T(256)S(1)}, s32[256]{0:T(256)S(1)}) all-reduce(s32[256]{0:T(256)S(1)} %dynamic-update-slice.6, s32[256]{0:T(256)S(1)} %bitcast_dynamic-update-slice_fusion), channel_id=1, replica_groups=mesh['elec'=64,'therm'=8] {'therm'}, use_global_device_ids=true, to_apply=%add | all-reduce | flops 512 | bytes 4096
  153.2 2.2 %gather_fusion.20 = bf16[128,64,128]{2,1,0:T(8,128)(2,1)} fusion(bf16[32,64,128]{2,1,0:T(8,128)(2,1)S(1)} %fusion.20, s32[1024]{0:T(1024)S(1)} %pad_clamp_fusion.5), kind=kCustom, calls=%fused_computation.20 | custom fusion | bytes 4194816 | tf_op jit(solution)/shard_map/gather | solution.py:36
  155.3 1.3 collective-permute-start.28
  157.6 3.1 %fusion.17 = bf16[32,64,128]{2,1,0:T(8,128)(2,1)S(1)} fusion(bf16[32,4,64,64]{3,2,1,0:T(8,128)(2,1)S(1)} %copy-done, bf16[32,4,64,128]{3,2,1,0:T(8,128)(2,1)} %bitcast.200, bf16[32,64,128]{2,1,0:T(8,128)(2,1)S(1)} %fusion.20, f32[32,64,128]{2,0,1:T(8,128)S(1)} %fusion.33, f32[32,64]{1,0:T(8,128)S(1)} %copy-done.8), kind=kOutput, calls=%fused_computation.59 | convolution fusion | flops 135790592 | bytes 5251072 | tf_op jit(solution)/shard_map/rkab,rkbc->rac/dot_general | solution.py:37
  160.6 4.6 %collective-permute-start.20 = (bf16[32,64,128]{2,1,0:T(8,128)(2,1)S(1)}, bf16[32,64,128]{2,1,0:T(8,128)(2,1)S(1)}, u32[]{:S(2)}, u32[]{:S(2)}) collective-permute-start(bf16[32,64,128]{2,1,0:T(8,128)(2,1)S(1)} %fusion.17), channel_id=1, source_target_pairs={{0,1},{1,2},{2,3},{3,4},{4,5},{5,6},{6,7},{7,0},{8,9},{9,10},{10,1... | collective-permute-start | bytes 1572872 | tf_op jit(solution)/shard_map/ppermute | solution.py:121
  165.5 2.5 %collective-permute-start.21 = (bf16[32,64,128]{2,1,0:T(8,128)(2,1)S(1)}, bf16[32,64,128]{2,1,0:T(8,128)(2,1)S(1)}, u32[]{:S(2)}, u32[]{:S(2)}) collective-permute-start(bf16[32,64,128]{2,1,0:T(8,128)(2,1)S(1)} %fusion.17), channel_id=1, source_target_pairs={{0,7},{1,0},{2,1},{3,2},{4,3},{5,4},{6,5},{7,6},{8,15},{9,8},{10,9... | collective-permute-start | bytes 1572872 | tf_op jit(solution)/shard_map/ppermute | solution.py:124
  168.0 1.7 fusion.79
  169.7 4.9 %collective-permute-done.20 = bf16[32,64,128]{2,1,0:T(8,128)(2,1)S(1)} collective-permute-done((bf16[32,64,128]{2,1,0:T(8,128)(2,1)S(1)}, bf16[32,64,128]{2,1,0:T(8,128)(2,1)S(1)}, u32[]{:S(2)}, u32[]{:S(2)}) %collective-permute-start.20) | collective-permute-done | bytes 524320 | tf_op jit(solution)/shard_map/ppermute | solution.py:121
  174.6 3.1 %collective-permute-start.22 = (bf16[32,64,128]{2,1,0:T(8,128)(2,1)S(1)}, bf16[32,64,128]{2,1,0:T(8,128)(2,1)S(1)}, u32[]{:S(2)}, u32[]{:S(2)}) collective-permute-start(bf16[32,64,128]{2,1,0:T(8,128)(2,1)S(1)} %collective-permute-done.20), channel_id=1, source_target_pairs={{0,1},{1,2},{2,3},{3,4},{4,5},{5,6},{6,7},{7,0},{8,9},{9,10},{10,1... | collective-permute-start | bytes 1572872 | tf_op jit(solution)/shard_map/ppermute | solution.py:121
  177.8 1.7 fusion.78
  179.4 4.0 %collective-permute-start.23 = (bf16[32,64,128]{2,1,0:T(8,128)(2,1)S(1)}, bf16[32,64,128]{2,1,0:T(8,128)(2,1)S(1)}, u32[]{:S(2)}, u32[]{:S(2)}) collective-permute-start(bf16[32,64,128]{2,1,0:T(8,128)(2,1)S(1)} %collective-permute-done.21), channel_id=1, source_target_pairs={{0,7},{1,0},{2,1},{3,2},{4,3},{5,4},{6,5},{7,6},{8,15},{9,8},{10,9... | collective-permute-start | bytes 1572872 | tf_op jit(solution)/shard_map/ppermute | solution.py:124
  183.4 1.0 broadcast_in_dim.7
  184.8 2.8 %collective-permute-done.22 = bf16[32,64,128]{2,1,0:T(8,128)(2,1)S(1)} collective-permute-done((bf16[32,64,128]{2,1,0:T(8,128)(2,1)S(1)}, bf16[32,64,128]{2,1,0:T(8,128)(2,1)S(1)}, u32[]{:S(2)}, u32[]{:S(2)}) %collective-permute-start.22) | collective-permute-done | bytes 524320 | tf_op jit(solution)/shard_map/ppermute | solution.py:121
  187.6 1.9 collective-permute-start.24
  190.3 1.1 collective-permute-done.23
  191.4 4.8 %collective-permute-start.25 = (bf16[32,64,128]{2,1,0:T(8,128)(2,1)S(1)}, bf16[32,64,128]{2,1,0:T(8,128)(2,1)S(1)}, u32[]{:S(2)}, u32[]{:S(2)}) collective-permute-start(bf16[32,64,128]{2,1,0:T(8,128)(2,1)S(1)} %collective-permute-done.23), channel_id=1, source_target_pairs={{0,7},{1,0},{2,1},{3,2},{4,3},{5,4},{6,5},{7,6},{8,15},{9,8},{10,9... | collective-permute-start | bytes 1572872 | tf_op jit(solution)/shard_map/ppermute | solution.py:124
  196.6 3.5 %collective-permute-done.24 = bf16[32,64,128]{2,1,0:T(8,128)(2,1)S(1)} collective-permute-done((bf16[32,64,128]{2,1,0:T(8,128)(2,1)S(1)}, bf16[32,64,128]{2,1,0:T(8,128)(2,1)S(1)}, u32[]{:S(2)}, u32[]{:S(2)}) %collective-permute-start.24) | collective-permute-done | bytes 524320 | tf_op jit(solution)/shard_map/ppermute | solution.py:121
  200.1 2.1 collective-permute-start.26
  203.4 9.0 %collective-permute-done.26 = bf16[32,64,128]{2,1,0:T(8,128)(2,1)S(1)} collective-permute-done((bf16[32,64,128]{2,1,0:T(8,128)(2,1)S(1)}, bf16[32,64,128]{2,1,0:T(8,128)(2,1)S(1)}, u32[]{:S(2)}, u32[]{:S(2)}) %collective-permute-start.26) | collective-permute-done | bytes 524320 | tf_op jit(solution)/shard_map/ppermute | solution.py:121
  212.8 1.0 convert_add_fusion
  213.7 1.6 copy.96
  (126 shorter events, 19.6 us)
Async XLA Ops:
  0.6 32.1 %copy-start = (bf16[32,4,64,64]{3,2,1,0:T(8,128)(2,1)S(1)}, bf16[32,4,64,64]{3,2,1,0:T(8,128)(2,1)}, u32[]{:S(2)}) copy-start(bf16[32,4,64,64]{3,2,1,0:T(8,128)(2,1)} %param.22) | copy-start | bytes 3145732
  0.6 27.7 %copy-start.10 = (s32[4,2]{0,1:T(2,128)S(1)}, s32[4,2]{0,1:T(2,128)}, u32[]{:S(2)}) copy-start(s32[4,2]{0,1:T(2,128)} %param.24) | copy-start | bytes 100
  0.7 27.4 %copy-start.13 = (s32[32,4]{0,1:T(4,128)S(1)}, s32[32,4]{0,1:T(4,128)}, u32[]{:S(2)}) copy-start(s32[32,4]{0,1:T(4,128)} %param.23) | copy-start | bytes 1540
  0.7 27.6 %copy-start.14 = (s32[32,3]{0,1:T(4,128)S(1)}, s32[32,3]{0,1:T(4,128)}, u32[]{:S(2)}) copy-start(s32[32,3]{0,1:T(4,128)} %param.31) | copy-start | bytes 1156
  3.7 27.1 %collective-permute-start = (bf16[2,64,128]{2,1,0:T(8,128)(2,1)S(1)}, bf16[2,64,128]{2,1,0:T(8,128)(2,1)S(1)}, u32[]{:S(2)}, u32[]{:S(2)}) collective-permute-start(bf16[2,64,128]{2,1,0:T(8,128)(2,1)S(1)} %gather_fusion.1), channel_id=1, source_target_pairs={{0,8},{8,0},{16,24},{24,16},{32,40},{40,32},{48,56},{56,48},{64,72... | collective-permute-start | bytes 98312 | tf_op jit(solution)/shard_map/ppermute | solution.py:19
  6.2 24.7 %collective-permute-start.1 = (bf16[2,64,128]{2,1,0:T(8,128)(2,1)S(1)}, bf16[2,64,128]{2,1,0:T(8,128)(2,1)S(1)}, u32[]{:S(2)}, u32[]{:S(2)}) collective-permute-start(bf16[2,64,128]{2,1,0:T(8,128)(2,1)S(1)} %gather_fusion.2), channel_id=1, source_target_pairs={{0,16},{16,0},{8,24},{24,8},{32,48},{48,32},{40,56},{56,40},{64,80... | collective-permute-start | bytes 98312 | tf_op jit(solution)/shard_map/ppermute | solution.py:19
  10.3 20.6 %collective-permute-start.2 = (bf16[2,64,128]{2,1,0:T(8,128)(2,1)S(1)}, bf16[2,64,128]{2,1,0:T(8,128)(2,1)}, u32[]{:S(2)}, u32[]{:S(2)}) collective-permute-start(bf16[2,64,128]{2,1,0:T(8,128)(2,1)S(1)} %gather_fusion.3), channel_id=1, source_target_pairs={{0,32},{32,0},{8,40},{40,8},{16,48},{48,16},{24,56},{56,24},{64,96... | collective-permute-start | bytes 98312 | tf_op jit(solution)/shard_map/ppermute | solution.py:19
  15.4 15.5 %collective-permute-start.3 = (bf16[2,64,128]{2,1,0:T(8,128)(2,1)S(1)}, bf16[2,64,128]{2,1,0:T(8,128)(2,1)}, u32[]{:S(2)}, u32[]{:S(2)}) collective-permute-start(bf16[2,64,128]{2,1,0:T(8,128)(2,1)S(1)} %gather_fusion.4), channel_id=1, source_target_pairs={{0,64},{64,0},{8,72},{72,8},{16,80},{80,16},{24,88},{88,24},{32,96... | collective-permute-start | bytes 98312 | tf_op jit(solution)/shard_map/ppermute | solution.py:19
  22.9 0.8 copy-start.3
  23.8 141.6 %collective-permute-start.27 = (bf16[2,64,128]{2,0,1:T(2,128)(2,1)S(1)}, bf16[2,64,128]{2,0,1:T(2,128)(2,1)S(1)}, u32[]{:S(2)}, u32[]{:S(2)}) collective-permute-start(bf16[2,64,128]{2,0,1:T(2,128)(2,1)S(1)} %get-tuple-element.39), channel_id=1, source_target_pairs={{0,1},{1,2},{2,3},{3,4},{4,5},{5,6},{6,7},{8,9},{9,10},{10,11},{11... | collective-permute-start | bytes 98312 | tf_op jit(solution)/shard_map/ppermute | solution.py:29
  28.5 4.2 %copy-start.7 = (bf16[32,64,128]{2,1,0:T(8,128)(2,1)S(1)}, bf16[32,64,128]{2,1,0:T(8,128)(2,1)}, u32[]{:S(2)}) copy-start(bf16[32,64,128]{2,1,0:T(8,128)(2,1)} %param.20) | copy-start | bytes 1572868
  28.5 4.2 %copy-start.8 = (f32[32,64]{1,0:T(8,128)S(1)}, f32[32,64]{1,0:T(8,128)}, u32[]{:S(2)}) copy-start(f32[32,64]{1,0:T(8,128)} %param.21) | copy-start | bytes 24580
  39.1 16.7 %collective-permute-start.4 = (bf16[2,64,128]{2,1,0:T(8,128)(2,1)S(1)}, bf16[2,64,128]{2,1,0:T(8,128)(2,1)S(1)}, u32[]{:S(2)}, u32[]{:S(2)}) collective-permute-start(bf16[2,64,128]{2,1,0:T(8,128)(2,1)S(1)} %gather_fusion.6), channel_id=1, source_target_pairs={{0,8},{8,0},{16,24},{24,16},{32,40},{40,32},{48,56},{56,48},{64,72... | collective-permute-start | bytes 98312 | tf_op jit(solution)/shard_map/ppermute | solution.py:19
  41.0 14.7 %collective-permute-start.5 = (bf16[2,64,128]{2,1,0:T(8,128)(2,1)S(1)}, bf16[2,64,128]{2,1,0:T(8,128)(2,1)S(1)}, u32[]{:S(2)}, u32[]{:S(2)}) collective-permute-start(bf16[2,64,128]{2,1,0:T(8,128)(2,1)S(1)} %gather_fusion.7), channel_id=1, source_target_pairs={{0,16},{16,0},{8,24},{24,8},{32,48},{48,32},{40,56},{56,40},{64,80... | collective-permute-start | bytes 98312 | tf_op jit(solution)/shard_map/ppermute | solution.py:19
  44.3 11.5 %collective-permute-start.6 = (bf16[2,64,128]{2,1,0:T(8,128)(2,1)S(1)}, bf16[2,64,128]{2,1,0:T(8,128)(2,1)}, u32[]{:S(2)}, u32[]{:S(2)}) collective-permute-start(bf16[2,64,128]{2,1,0:T(8,128)(2,1)S(1)} %gather_fusion.8), channel_id=1, source_target_pairs={{0,32},{32,0},{8,40},{40,8},{16,48},{48,16},{24,56},{56,24},{64,96... | collective-permute-start | bytes 98312 | tf_op jit(solution)/shard_map/ppermute | solution.py:19
  48.3 10.1 %collective-permute-start.7 = (bf16[2,64,128]{2,1,0:T(8,128)(2,1)S(1)}, bf16[2,64,128]{2,1,0:T(8,128)(2,1)}, u32[]{:S(2)}, u32[]{:S(2)}) collective-permute-start(bf16[2,64,128]{2,1,0:T(8,128)(2,1)S(1)} %gather_fusion.9), channel_id=1, source_target_pairs={{0,64},{64,0},{8,72},{72,8},{16,80},{80,16},{24,88},{88,24},{32,96... | collective-permute-start | bytes 98312 | tf_op jit(solution)/shard_map/ppermute | solution.py:19
  53.6 4.8 %copy-start.15 = (bf16[8,64,64]{2,1,0:T(8,128)(2,1)S(1)}, bf16[8,64,64]{2,1,0:T(8,128)(2,1)}, u32[]{:S(2)}) copy-start(bf16[8,64,64]{2,1,0:T(8,128)(2,1)} %param.25) | copy-start | bytes 196612
  64.6 18.3 %copy-start.2 = (bf16[32,64,128]{2,1,0:T(8,128)(2,1)}, bf16[32,64,128]{2,1,0:T(8,128)(2,1)S(1)}, u32[]{:S(2)}) copy-start(bf16[32,64,128]{2,1,0:T(8,128)(2,1)S(1)} %get-tuple-element.42) | copy-start | bytes 1572868
  66.8 18.2 %collective-permute-start.10 = (bf16[2,64,128]{2,1,0:T(8,128)(2,1)S(1)}, bf16[2,64,128]{2,1,0:T(8,128)(2,1)S(1)}, u32[]{:S(2)}, u32[]{:S(2)}) collective-permute-start(bf16[2,64,128]{2,1,0:T(8,128)(2,1)S(1)} %gather_fusion.13), channel_id=1, source_target_pairs={{0,32},{32,0},{8,40},{40,8},{16,48},{48,16},{24,56},{56,24},{64,96... | collective-permute-start | bytes 98312 | tf_op jit(solution)/shard_map/ppermute | solution.py:19
  69.3 15.8 %collective-permute-start.8 = (bf16[2,64,128]{2,1,0:T(8,128)(2,1)S(1)}, bf16[2,64,128]{2,1,0:T(8,128)(2,1)S(1)}, u32[]{:S(2)}, u32[]{:S(2)}) collective-permute-start(bf16[2,64,128]{2,1,0:T(8,128)(2,1)S(1)} %gather_fusion.11), channel_id=1, source_target_pairs={{0,8},{8,0},{16,24},{24,16},{32,40},{40,32},{48,56},{56,48},{64,72... | collective-permute-start | bytes 98312 | tf_op jit(solution)/shard_map/ppermute | solution.py:19
  71.2 13.8 %collective-permute-start.9 = (bf16[2,64,128]{2,1,0:T(8,128)(2,1)S(1)}, bf16[2,64,128]{2,1,0:T(8,128)(2,1)S(1)}, u32[]{:S(2)}, u32[]{:S(2)}) collective-permute-start(bf16[2,64,128]{2,1,0:T(8,128)(2,1)S(1)} %gather_fusion.12), channel_id=1, source_target_pairs={{0,16},{16,0},{8,24},{24,8},{32,48},{48,32},{40,56},{56,40},{64,80... | collective-permute-start | bytes 98312 | tf_op jit(solution)/shard_map/ppermute | solution.py:19
  74.2 10.9 %collective-permute-start.11 = (bf16[2,64,128]{2,1,0:T(8,128)(2,1)S(1)}, bf16[2,64,128]{2,1,0:T(8,128)(2,1)S(1)}, u32[]{:S(2)}, u32[]{:S(2)}) collective-permute-start(bf16[2,64,128]{2,1,0:T(8,128)(2,1)S(1)} %gather_fusion.14), channel_id=1, source_target_pairs={{0,64},{64,0},{8,72},{72,8},{16,80},{80,16},{24,88},{88,24},{32,96... | collective-permute-start | bytes 98312 | tf_op jit(solution)/shard_map/ppermute | solution.py:19
  79.2 3.6 %copy-start.11 = (f32[32,64]{1,0:T(8,128)S(1)}, f32[32,64]{1,0:T(8,128)}, u32[]{:S(2)}) copy-start(f32[32,64]{1,0:T(8,128)} %param.29) | copy-start | bytes 24580
  82.8 2.2 %copy-start.16 = (bf16[8,64,64]{2,1,0:T(8,128)(2,1)S(1)}, bf16[8,64,64]{2,1,0:T(8,128)(2,1)}, u32[]{:S(2)}) copy-start(bf16[8,64,64]{2,1,0:T(8,128)(2,1)} %param.25) | copy-start | bytes 196612
  85.9 21.1 %copy-start.4 = (bf16[32,64,128]{2,1,0:T(8,128)(2,1)S(1)}, bf16[32,64,128]{2,1,0:T(8,128)(2,1)}, u32[]{:S(2)}) copy-start(bf16[32,64,128]{2,1,0:T(8,128)(2,1)} %param.28) | copy-start | bytes 1572868
  92.9 22.1 %collective-permute-start.12 = (bf16[2,64,128]{2,1,0:T(8,128)(2,1)S(1)}, bf16[2,64,128]{2,1,0:T(8,128)(2,1)S(1)}, u32[]{:S(2)}, u32[]{:S(2)}) collective-permute-start(bf16[2,64,128]{2,1,0:T(8,128)(2,1)S(1)} %gather_fusion.16), channel_id=1, source_target_pairs={{0,8},{8,0},{16,24},{24,16},{32,40},{40,32},{48,56},{56,48},{64,72... | collective-permute-start | bytes 98312 | tf_op jit(solution)/shard_map/ppermute | solution.py:19
  94.8 20.1 %collective-permute-start.13 = (bf16[2,64,128]{2,1,0:T(8,128)(2,1)S(1)}, bf16[2,64,128]{2,1,0:T(8,128)(2,1)S(1)}, u32[]{:S(2)}, u32[]{:S(2)}) collective-permute-start(bf16[2,64,128]{2,1,0:T(8,128)(2,1)S(1)} %gather_fusion.17), channel_id=1, source_target_pairs={{0,16},{16,0},{8,24},{24,8},{32,48},{48,32},{40,56},{56,40},{64,80... | collective-permute-start | bytes 98312 | tf_op jit(solution)/shard_map/ppermute | solution.py:19
  98.1 16.9 %collective-permute-start.14 = (bf16[2,64,128]{2,1,0:T(8,128)(2,1)S(1)}, bf16[2,64,128]{2,1,0:T(8,128)(2,1)}, u32[]{:S(2)}, u32[]{:S(2)}) collective-permute-start(bf16[2,64,128]{2,1,0:T(8,128)(2,1)S(1)} %gather_fusion.18), channel_id=1, source_target_pairs={{0,32},{32,0},{8,40},{40,8},{16,48},{48,16},{24,56},{56,24},{64,96... | collective-permute-start | bytes 98312 | tf_op jit(solution)/shard_map/ppermute | solution.py:19
  102.2 12.8 %collective-permute-start.15 = (bf16[2,64,128]{2,1,0:T(8,128)(2,1)S(1)}, bf16[2,64,128]{2,1,0:T(8,128)(2,1)}, u32[]{:S(2)}, u32[]{:S(2)}) collective-permute-start(bf16[2,64,128]{2,1,0:T(8,128)(2,1)S(1)} %gather_fusion.19), channel_id=1, source_target_pairs={{0,64},{64,0},{8,72},{72,8},{16,80},{80,16},{24,88},{88,24},{32,96... | collective-permute-start | bytes 98312 | tf_op jit(solution)/shard_map/ppermute | solution.py:19
  112.8 2.2 %copy-start.17 = (bf16[8,64,64]{2,1,0:T(8,128)(2,1)S(1)}, bf16[8,64,64]{2,1,0:T(8,128)(2,1)}, u32[]{:S(2)}) copy-start(bf16[8,64,64]{2,1,0:T(8,128)(2,1)} %param.25) | copy-start | bytes 196612
  116.7 18.2 %copy-start.19 = (s32[32,1]{0,1:T(1,128)S(1)}, s32[32,1]{0,1:T(1,128)}, u32[]{:S(2)}) copy-start(s32[32,1]{0,1:T(1,128)} %param.26) | copy-start | bytes 388
  116.7 18.3 %copy-start.20 = (s32[32]{0:T(128)S(1)}, s32[32]{0:T(128)}, u32[]{:S(2)}) copy-start(s32[32]{0:T(128)} %param.27) | copy-start | bytes 388
  120.2 37.3 %copy-start.1 = (bf16[32,64,128]{2,1,0:T(8,128)(2,1)}, bf16[32,64,128]{2,1,0:T(8,128)(2,1)S(1)}, u32[]{:S(2)}) copy-start(bf16[32,64,128]{2,1,0:T(8,128)(2,1)S(1)} %fusion.20) | copy-start | bytes 1572868
  122.5 32.8 %collective-permute-start.16 = (bf16[2,64,128]{2,1,0:T(8,128)(2,1)S(1)}, bf16[2,64,128]{2,1,0:T(8,128)(2,1)S(1)}, u32[]{:S(2)}, u32[]{:S(2)}) collective-permute-start(bf16[2,64,128]{2,1,0:T(8,128)(2,1)S(1)} %gather_fusion.21), channel_id=1, source_target_pairs={{0,8},{8,0},{16,24},{24,16},{32,40},{40,32},{48,56},{56,48},{64,72... | collective-permute-start | bytes 98312 | tf_op jit(solution)/shard_map/ppermute | solution.py:19
  124.4 32.2 %collective-permute-start.17 = (bf16[2,64,128]{2,1,0:T(8,128)(2,1)S(1)}, bf16[2,64,128]{2,1,0:T(8,128)(2,1)S(1)}, u32[]{:S(2)}, u32[]{:S(2)}) collective-permute-start(bf16[2,64,128]{2,1,0:T(8,128)(2,1)S(1)} %gather_fusion.22), channel_id=1, source_target_pairs={{0,16},{16,0},{8,24},{24,8},{32,48},{48,32},{40,56},{56,40},{64,80... | collective-permute-start | bytes 98312 | tf_op jit(solution)/shard_map/ppermute | solution.py:19
  127.1 29.6 %collective-permute-start.18 = (bf16[2,64,128]{2,1,0:T(8,128)(2,1)S(1)}, bf16[2,64,128]{2,1,0:T(8,128)(2,1)S(1)}, u32[]{:S(2)}, u32[]{:S(2)}) collective-permute-start(bf16[2,64,128]{2,1,0:T(8,128)(2,1)S(1)} %gather_fusion.23), channel_id=1, source_target_pairs={{0,32},{32,0},{8,40},{40,8},{16,48},{48,16},{24,56},{56,24},{64,96... | collective-permute-start | bytes 98312 | tf_op jit(solution)/shard_map/ppermute | solution.py:19
  129.8 26.8 %collective-permute-start.19 = (bf16[2,64,128]{2,1,0:T(8,128)(2,1)S(1)}, bf16[2,64,128]{2,1,0:T(8,128)(2,1)S(1)}, u32[]{:S(2)}, u32[]{:S(2)}) collective-permute-start(bf16[2,64,128]{2,1,0:T(8,128)(2,1)S(1)} %gather_fusion.24), channel_id=1, source_target_pairs={{0,64},{64,0},{8,72},{72,8},{16,80},{80,16},{24,88},{88,24},{32,96... | collective-permute-start | bytes 98312 | tf_op jit(solution)/shard_map/ppermute | solution.py:19
  153.2 3.5 %copy-start.18 = (bf16[8,64,64]{2,1,0:T(8,128)(2,1)S(1)}, bf16[8,64,64]{2,1,0:T(8,128)(2,1)}, u32[]{:S(2)}) copy-start(bf16[8,64,64]{2,1,0:T(8,128)(2,1)} %param.25) | copy-start | bytes 196612
  155.3 22.3 %collective-permute-start.28 = (bf16[2,64,128]{2,0,1:T(2,128)(2,1)S(1)}, bf16[2,64,128]{2,0,1:T(2,128)(2,1)S(1)}, u32[]{:S(2)}, u32[]{:S(2)}) collective-permute-start(bf16[2,64,128]{2,0,1:T(2,128)(2,1)S(1)} %get-tuple-element.38), channel_id=1, source_target_pairs={{1,0},{2,1},{3,2},{4,3},{5,4},{6,5},{7,6},{9,8},{10,9},{11,10},{12... | collective-permute-start | bytes 98312 | tf_op jit(solution)/shard_map/ppermute | solution.py:30
  157.5 7.8 %copy-start.12 = (f32[32,64]{1,0:T(8,128)S(1)}, f32[32,64]{1,0:T(8,128)}, u32[]{:S(2)}) copy-start(f32[32,64]{1,0:T(8,128)} %param.35) | copy-start | bytes 24580
  157.5 7.9 %copy-start.9 = (bf16[4,64,64]{2,1,0:T(8,128)(2,1)S(1)}, bf16[4,64,64]{2,1,0:T(8,128)(2,1)}, u32[]{:S(2)}) copy-start(bf16[4,64,64]{2,1,0:T(8,128)(2,1)} %param.32) | copy-start | bytes 98308
  160.6 14.0 %collective-permute-start.20 = (bf16[32,64,128]{2,1,0:T(8,128)(2,1)S(1)}, bf16[32,64,128]{2,1,0:T(8,128)(2,1)S(1)}, u32[]{:S(2)}, u32[]{:S(2)}) collective-permute-start(bf16[32,64,128]{2,1,0:T(8,128)(2,1)S(1)} %fusion.17), channel_id=1, source_target_pairs={{0,1},{1,2},{2,3},{3,4},{4,5},{5,6},{6,7},{7,0},{8,9},{9,10},{10,1... | collective-permute-start | bytes 1572872 | tf_op jit(solution)/shard_map/ppermute | solution.py:121
  165.5 13.9 %collective-permute-start.21 = (bf16[32,64,128]{2,1,0:T(8,128)(2,1)S(1)}, bf16[32,64,128]{2,1,0:T(8,128)(2,1)S(1)}, u32[]{:S(2)}, u32[]{:S(2)}) collective-permute-start(bf16[32,64,128]{2,1,0:T(8,128)(2,1)S(1)} %fusion.17), channel_id=1, source_target_pairs={{0,7},{1,0},{2,1},{3,2},{4,3},{5,4},{6,5},{7,6},{8,15},{9,8},{10,9... | collective-permute-start | bytes 1572872 | tf_op jit(solution)/shard_map/ppermute | solution.py:124
  174.6 13.0 %collective-permute-start.22 = (bf16[32,64,128]{2,1,0:T(8,128)(2,1)S(1)}, bf16[32,64,128]{2,1,0:T(8,128)(2,1)S(1)}, u32[]{:S(2)}, u32[]{:S(2)}) collective-permute-start(bf16[32,64,128]{2,1,0:T(8,128)(2,1)S(1)} %collective-permute-done.20), channel_id=1, source_target_pairs={{0,1},{1,2},{2,3},{3,4},{4,5},{5,6},{6,7},{7,0},{8,9},{9,10},{10,1... | collective-permute-start | bytes 1572872 | tf_op jit(solution)/shard_map/ppermute | solution.py:121
  179.4 11.9 %collective-permute-start.23 = (bf16[32,64,128]{2,1,0:T(8,128)(2,1)S(1)}, bf16[32,64,128]{2,1,0:T(8,128)(2,1)S(1)}, u32[]{:S(2)}, u32[]{:S(2)}) collective-permute-start(bf16[32,64,128]{2,1,0:T(8,128)(2,1)S(1)} %collective-permute-done.21), channel_id=1, source_target_pairs={{0,7},{1,0},{2,1},{3,2},{4,3},{5,4},{6,5},{7,6},{8,15},{9,8},{10,9... | collective-permute-start | bytes 1572872 | tf_op jit(solution)/shard_map/ppermute | solution.py:124
  187.6 12.5 %collective-permute-start.24 = (bf16[32,64,128]{2,1,0:T(8,128)(2,1)S(1)}, bf16[32,64,128]{2,1,0:T(8,128)(2,1)S(1)}, u32[]{:S(2)}, u32[]{:S(2)}) collective-permute-start(bf16[32,64,128]{2,1,0:T(8,128)(2,1)S(1)} %collective-permute-done.22), channel_id=1, source_target_pairs={{0,1},{1,2},{2,3},{3,4},{4,5},{5,6},{6,7},{7,0},{8,9},{9,10},{10,1... | collective-permute-start | bytes 1572872 | tf_op jit(solution)/shard_map/ppermute | solution.py:121
  191.4 11.6 %collective-permute-start.25 = (bf16[32,64,128]{2,1,0:T(8,128)(2,1)S(1)}, bf16[32,64,128]{2,1,0:T(8,128)(2,1)S(1)}, u32[]{:S(2)}, u32[]{:S(2)}) collective-permute-start(bf16[32,64,128]{2,1,0:T(8,128)(2,1)S(1)} %collective-permute-done.23), channel_id=1, source_target_pairs={{0,7},{1,0},{2,1},{3,2},{4,3},{5,4},{6,5},{7,6},{8,15},{9,8},{10,9... | collective-permute-start | bytes 1572872 | tf_op jit(solution)/shard_map/ppermute | solution.py:124
  196.6 16.2 %copy-start.5 = (bf16[32,64,128]{2,1,0:T(8,128)(2,1)S(1)}, bf16[32,64,128]{2,1,0:T(8,128)(2,1)}, u32[]{:S(2)}) copy-start(bf16[32,64,128]{2,1,0:T(8,128)(2,1)} %param.28) | copy-start | bytes 1572868
  196.6 16.2 %copy-start.6 = (f32[32,64,128]{2,0,1:T(8,128)S(1)}, f32[32,64,128]{2,0,1:T(8,128)}, u32[]{:S(2)}) copy-start(f32[32,64,128]{2,0,1:T(8,128)} %fusion.78) | copy-start | bytes 3145732
  200.1 12.3 %collective-permute-start.26 = (bf16[32,64,128]{2,1,0:T(8,128)(2,1)S(1)}, bf16[32,64,128]{2,1,0:T(8,128)(2,1)S(1)}, u32[]{:S(2)}, u32[]{:S(2)}) collective-permute-start(bf16[32,64,128]{2,1,0:T(8,128)(2,1)S(1)} %collective-permute-done.24), channel_id=1, source_target_pairs={{0,1},{1,2},{2,3},{3,4},{4,5},{5,6},{6,7},{7,0},{8,9},{9,10},{10,1... | collective-permute-start | bytes 1572872 | tf_op jit(solution)/shard_map/ppermute | solution.py:121
